TPU v7x, 256 devices: a whole 4x4x8 slice. The times are simulated.
256 devices in a mesh: leaf: 256 (over y, x, z, core).
Axes of the slice: x: 4, y: 4, z: 8, core: 2. Of those that a mesh axis runs over, the one named last changes fastest.
Arguments:
- points: float32 [28, 524288], P(None, 'leaf'), may hold values from -3 to 3
- tree_order: int32 [256, 2048], P('leaf'), may hold values from 0 to 2047, each once within a row
- leaf_basis: bfloat16 [1024, 512, 256], P('leaf'), may hold values from -0.25 to 0.25
- local_transfer: bfloat16 [1792, 256, 256], P('leaf'), may hold values from -0.2651875 to 0.2651875
- local_coupling: bfloat16 [768, 256, 256], P('leaf'), may hold values from -0.375 to 0.375
- device_transfer: bfloat16 [256, 6, 256, 256], P('leaf'), may hold values from -0.2651875 to 0.2651875, as said below
- device_coupling: bfloat16 [256, 8, 256, 256], P('leaf'), may hold values from -5.091169 to 5.091169, as said below
- solution: float32 [524288, 128], P('leaf'), may hold values from -6 to 6
- residual: float32 [524288, 128], P('leaf'), may hold values from -40 to 40
- direction: float32 [524288, 128], P('leaf'), may hold values from -40 to 40
Outputs:
- new_solution: float32 [524288, 128], P('leaf')
- new_residual: float32 [524288, 128], P('leaf')
- new_direction: float32 [524288, 128], P('leaf')
Inputs may be any that keep to these rules, and one draw needn't show every extreme that they name: `tree_order`: each row is a permutation of 0 to 2047. `device_transfer`: entry m - 1 of a device is the transfer matrix of its ancestor node that spans 2 ** m devices; every device under that node holds the same matrix. `device_coupling`: entry m of a device is the coupling matrix that multiplies the coefficients of the sibling of its ancestor spanning 2 ** m devices; the devices of the lower side hold B, those of the upper side its transpose.
All inputs are finite; a program needn't handle non-finite values.
Results may differ from a plain program's by a relative error of at most 0.035.
Values may be sent and summed in bfloat16 or wider, within the bound.
No kernel may reach another device: no remote copies, remote signals or barrier semaphores. Data moves between devices by JAX's collectives and lax.ppermute only.
A program may use at most 64 MiB of HBM per device.

v0:
```python
import functools

import jax
import jax.numpy as jnp
from jax import lax
from jax.experimental import pallas as pl
from jax.experimental.pallas import tpu as pltpu
from jax.sharding import PartitionSpec as P

ITERATIONS = 3
ridge_weight = 32.0
sharpness = 0.25
LEAVES = 4
ROWS = 512
RANK = 256
COLS = 128
LEVELS = 8
PAYLOAD = RANK + 16
BF = jnp.bfloat16
F32 = jnp.float32


def dot(left, right):
    return jnp.dot(left, right, preferred_element_type=F32)


def params(size=16 << 20):
    return pltpu.CompilerParams(vmem_limit_bytes=size)


in_vmem = pl.BlockSpec(memory_space=pltpu.VMEM)


def whole(shape):
    return pl.BlockSpec(shape, lambda *_: (0,) * len(shape))


def partners(count):
    turn = {0: 6, 1: 7, 2: 4, 3: 5, 4: 2, 5: 3, 6: 0, 7: 1}
    levels = []
    for level in range(count.bit_length() - 1):
        pairs = []
        for i in range(count):
            if level == 3:
                j = i & ~14 | turn[i >> 1 & 7] << 1
            elif level in (5, 7):
                j = i ^ 3 << level - 1
            else:
                j = i ^ 1 << level
            pairs.append((i, j))
        levels.append(pairs)
    return levels


def split3(value):
    high = value.astype(BF)
    rest = value - high.astype(F32)
    mid = rest.astype(BF)
    low = (rest - mid.astype(F32)).astype(BF)
    return high, mid, low


def pack_sums(sums):
    high, mid, _ = split3(sums)
    return jnp.concatenate([high.astype(F32), mid.astype(F32)], axis=0).astype(BF)


def unpack_sums(packed):
    wide = packed.astype(F32)
    return wide[0:8] + wide[8:16]


def row_of(sums, index):
    return sums[index : index + 1]


def stack_rows(*rows):
    place = lax.broadcasted_iota(jnp.int32, (8, COLS), 0)
    total = jnp.zeros((8, COLS), F32)
    for index, row in enumerate(rows):
        total = total + jnp.where(place == index, row, 0.0)
    return total


def call(kernel, name, operands, shapes):
    return pl.pallas_call(
        kernel,
        in_specs=[in_vmem] * len(operands),
        out_specs=[in_vmem] * len(shapes),
        out_shape=shapes,
        compiler_params=params(),
        name=name,
    )(*operands)


def rows8(*rows):
    place = lax.broadcasted_iota(jnp.int32, (8, rows[0].shape[1]), 0)
    block = jnp.zeros(place.shape, F32)
    for index, row in enumerate(rows):
        block = block + jnp.where(place == index, row, 0.0)
    return block


def leaf_kernel(points_ref, order_ref, out_ref):
    value = points_ref[...]
    total = value.shape[1]
    gap = jnp.zeros((4, total), F32)
    pieces = []
    for piece in split3(value):
        pieces += [piece.astype(F32), gap]
    pieces = jnp.concatenate(pieces, axis=0).astype(BF)
    place = lax.broadcasted_iota(jnp.int32, (total, ROWS), 0)
    for i in range(LEAVES):
        picked = order_ref[:, i * ROWS : (i + 1) * ROWS]
        chosen = jnp.where(place == picked, 1.0, 0.0).astype(BF)
        moved = dot(pieces, chosen)
        high, mid, low = moved[0:32], moved[32:64], moved[64:96]
        full = high + mid + low
        half = -0.5 * jnp.sum(full * full, axis=0, keepdims=True)
        h3, m3, l3 = (piece.astype(F32) for piece in split3(half))
        one = jnp.ones_like(half)
        pad = jnp.zeros((8, ROWS), F32)
        left = jnp.concatenate(
            [high, high, mid, high, low, mid, rows8(h3, m3, l3, one, one, one), pad], axis=0
        ).astype(BF)
        right = jnp.concatenate(
            [high, mid, high, low, high, mid, rows8(one, one, one, h3, m3, l3), pad], axis=0
        ).astype(BF)
        inner = lax.dot_general(
            left, right, (((0,), (0,)), ((), ())), preferred_element_type=F32
        )
        out_ref[i] = jnp.exp((2.0 * sharpness) * inner).astype(BF)


def make_kernels(points, order):
    total = points.shape[1]
    return pl.pallas_call(
        leaf_kernel,
        in_specs=[in_vmem, in_vmem],
        out_specs=in_vmem,
        out_shape=jax.ShapeDtypeStruct((LEAVES, ROWS, ROWS), BF),
        compiler_params=params(),
        cost_estimate=pl.CostEstimate(
            flops=2 * LEAVES * (96 * total + 208 * ROWS) * ROWS,
            bytes_accessed=4 << 20,
            transcendentals=LEAVES * ROWS * ROWS,
        ),
        name="leaf_kernels",
    )(points, order)


def compose_kernel(basis, local_r, local_b, tall, mix, paths):
    first = [local_r[i] for i in range(LEAVES)]
    second = [local_r[LEAVES], local_r[LEAVES + 1]]
    flipped = [block.T for block in first]
    pair = local_b[2]
    across = [pair, pair.T]
    below = LEAVES * RANK
    for i in range(LEAVES):
        tall[i] = basis[i].T
        path = dot(first[i], second[i // 2]).astype(BF)
        paths[i * RANK : (i + 1) * RANK] = path
        mix[below:, i * RANK : (i + 1) * RANK] = path.T
        side = dot(first[i], across[i // 2]).astype(BF)
        for j in range(LEAVES):
            if i == j:
                block = jnp.zeros((RANK, RANK), BF)
            elif i // 2 == j // 2:
                block = local_b[i // 2]
                if i % 2:
                    block = block.T
            else:
                block = dot(side, flipped[j]).astype(BF)
            mix[i * RANK : (i + 1) * RANK, j * RANK : (j + 1) * RANK] = block


def compose(basis, local_r, local_b):
    shapes = [
        (LEAVES, RANK, ROWS),
        ((LEAVES + 1) * RANK, LEAVES * RANK),
        (LEAVES * RANK, RANK),
    ]
    return call(
        compose_kernel,
        "compose",
        (basis, local_r, local_b),
        [jax.ShapeDtypeStruct(shape, BF) for shape in shapes],
    )


def descend_kernel(local_r, device_r, device_b, down):
    path = None
    for level in range(LEVELS):
        coupling = device_b[0, level]
        down[level, :RANK, :] = coupling
        if path is None:
            down[level, RANK:, :] = coupling
        else:
            down[level, RANK:, :] = dot(path, coupling).astype(BF)
        if level + 1 < LEVELS:
            step = local_r[LEAVES + 2] if level == 0 else device_r[0, level - 1]
            path = step if path is None else dot(path, step).astype(BF)


def descend(local_r, device_r, device_b):
    return call(
        descend_kernel,
        "descend",
        (local_r, device_r, device_b),
        [jax.ShapeDtypeStruct((LEVELS, 2 * RANK, RANK), BF)],
    )[0]


def flip_kernel(local_r, device_r, *rest):
    out = rest[-1]
    for level in range(LEVELS - 1):
        step = local_r[LEAVES + 2] if level == 0 else device_r[0, level - 1]
        out[level, :, :RANK] = step.T
        out[level, :, RANK:] = rest[level][...].T


def flip(local_r, device_r, other_r):
    return pl.pallas_call(
        flip_kernel,
        in_specs=[in_vmem] * (2 + len(other_r)),
        out_specs=in_vmem,
        out_shape=jax.ShapeDtypeStruct((LEVELS - 1, RANK, 2 * RANK), BF),
        compiler_params=params(),
        name="flip",
    )(local_r, device_r, *other_r)


def climb_kernel(level, own, got, up, down, *rest):
    field_in = rest[0] if level else None
    out, field_out = rest[-2:]
    mine = own[:RANK]
    theirs = got[:RANK]
    out[:RANK] = dot(up[level], jnp.concatenate([mine, theirs], axis=0)).astype(BF)
    felt = dot(down[level], theirs)
    energy = jnp.sum(mine.astype(F32) * felt[:RANK], axis=0, keepdims=True)
    zero = jnp.zeros_like(energy)
    sums = unpack_sums(own[RANK:]) + unpack_sums(got[RANK:])
    out[RANK:] = pack_sums(sums + stack_rows(zero, 2.0 * energy))
    if level:
        field_out[...] = field_in[...] + felt[RANK:]
    else:
        field_out[...] = felt[RANK:]


def climb(level, own, got, up, down, field):
    operands = [own, got, up, down] + ([field] if level else [])
    return pl.pallas_call(
        functools.partial(climb_kernel, level),
        in_specs=[in_vmem] * len(operands),
        out_specs=[in_vmem] * 2,
        out_shape=[payload_shape, field_shape],
        compiler_params=params(4 << 20),
        name="climb",
    )(*operands)


def finish_sweep(own, got, down, field_in, scalars_in, first):
    mine = own[:RANK]
    theirs = got[:RANK]
    felt = dot(down[LEVELS - 1], theirs)
    field = (field_in[...] + felt[RANK:]).astype(BF)
    energy = jnp.sum(mine.astype(F32) * felt[:RANK], axis=0, keepdims=True)
    sums = unpack_sums(own[RANK:]) + unpack_sums(got[RANK:])
    norm = row_of(sums, 0)
    curve = row_of(sums, 1) + 2.0 * energy
    if first:
        return field, norm, curve, norm / curve, None
    turn = norm / scalars_in[0:1]
    bend = curve + turn * (2.0 * row_of(sums, 2) + turn * scalars_in[1:2])
    return field, norm, bend, norm / bend, turn


def column_sum(value):
    return jnp.sum(value, axis=0, keepdims=True)


def leaf_apply(vector, kernel, tall):
    low = vector.astype(BF)
    return dot(kernel, low) + ridge_weight * vector, dot(tall, low).astype(BF)


def close_leaves(mix, gathered, sums, near, payload):
    packed = jnp.concatenate(gathered, axis=0)
    below = LEAVES * RANK
    payload[:RANK] = dot(mix[below:], packed).astype(BF)
    felt = dot(mix[:below], packed)
    energy = column_sum(packed.astype(F32) * felt)
    near[...] = felt
    payload[RANK:] = pack_sums(sums + stack_rows(jnp.zeros_like(energy), energy))


def begin_kernel(residual, direction, kernel, tall, mix, base, near, payload):
    sums = None
    gathered = []
    for i in range(LEAVES):
        rows = slice(i * ROWS, (i + 1) * ROWS)
        vector = direction[rows]
        out, local = leaf_apply(vector, kernel[i], tall[i])
        base[rows] = out
        here = residual[rows]
        part = stack_rows(column_sum(here * here), column_sum(vector * out))
        sums = part if i == 0 else sums + part
        gathered.append(local)
    close_leaves(mix, gathered, sums, near, payload)


def leaf_fields(paths, near, field):
    every = (near[...] + dot(paths[...], field)).astype(BF)
    return [every[i * RANK : (i + 1) * RANK] for i in range(LEAVES)]


def turn_kernel(first, own, got, down, field_in, scalars_in, *rest):
    basis, paths, base_in, near_in = rest[:4]
    rest = rest[4:]
    if first:
        residual, image, kernel, tall, mix = rest[:5]
        residual_out, image_out, base, near, payload, scalars = rest[5:]
    else:
        residual, direction, image, kernel, tall, mix = rest[:6]
        residual_out, direction_out, image_out, base, near, payload, scalars = rest[6:]
    field, norm, bend, size, beta = finish_sweep(own, got, down, field_in, scalars_in, first)
    scalars[...] = stack_rows(norm, bend, size)
    fields = leaf_fields(paths, near_in, field)
    sums = None
    gathered = []
    for i in range(LEAVES):
        rows = slice(i * ROWS, (i + 1) * ROWS)
        pushed = base_in[rows] + dot(basis[i], fields[i])
        here = residual[rows]
        if not first:
            pushed = pushed + beta * image[rows]
            direction_out[rows] = here + beta * direction[rows]
        here = here - size * pushed
        residual_out[rows] = here
        image_out[rows] = pushed
        out, local = leaf_apply(here, kernel[i], tall[i])
        base[rows] = out
        part = stack_rows(column_sum(here * here), column_sum(here * out), column_sum(here * pushed))
        sums = part if i == 0 else sums + part
        gathered.append(local)
    close_leaves(mix, gathered, sums, near, payload)


def end_kernel(
    own,
    got,
    down,
    field_in,
    scalars_in,
    basis,
    paths,
    base_in,
    near_in,
    residual,
    direction,
    image,
    solved,
    residual_out,
    residual_kept,
    direction_out,
    solved_out,
    scalars,
    sums_out,
):
    field, norm, bend, size, beta = finish_sweep(own, got, down, field_in, scalars_in, False)
    scalars[...] = stack_rows(norm, bend, size)
    fields = leaf_fields(paths, near_in, field)
    sums = None
    for i in range(LEAVES):
        rows = slice(i * ROWS, (i + 1) * ROWS)
        pushed = base_in[rows] + dot(basis[i], fields[i])
        pushed = pushed + beta * image[rows]
        here = residual[rows]
        step = here + beta * direction[rows]
        direction_out[rows] = step
        solved_out[rows] = solved[rows] + size * step
        here = here - size * pushed
        residual_out[rows] = here
        residual_kept[rows] = here
        part = column_sum(here * here)
        sums = part if i == 0 else sums + part
    sums_out[...] = jnp.broadcast_to(sums, sums_out.shape)


def last_kernel(parts, residual, direction, scalars, out):
    beta = column_sum(parts[...]) / scalars[0:1]
    out[...] = residual[...] + beta * direction[...]


vector_shape = jax.ShapeDtypeStruct((LEAVES * ROWS, COLS), F32)
near_shape = jax.ShapeDtypeStruct((LEAVES * RANK, COLS), F32)
payload_shape = jax.ShapeDtypeStruct((PAYLOAD, COLS), BF)
field_shape = jax.ShapeDtypeStruct((RANK, COLS), F32)
small_shape = jax.ShapeDtypeStruct((8, COLS), F32)


def begin(residual, direction, kernels, tall, mix):
    return call(
        begin_kernel,
        "begin",
        (residual, direction, kernels, tall, mix),
        [vector_shape, near_shape, payload_shape],
    )


def turn(first, sweep, scalars, leaves, residual, direction, image, apply):
    vectors = (residual, image) if first else (residual, direction, image)
    results = call(
        functools.partial(turn_kernel, first),
        "turn",
        (*sweep, scalars, *leaves, *vectors, *apply),
        [vector_shape] * (len(vectors) + 1) + [near_shape, payload_shape, small_shape],
    )
    if first:
        return results[0], direction, *results[1:]
    return results


def end(sweep, scalars, leaves, residual, direction, image, solved, count):
    return call(
        end_kernel,
        "end",
        (*sweep, scalars, *leaves, residual, direction, image, solved),
        [vector_shape] * 4 + [small_shape, jax.ShapeDtypeStruct((count, COLS), F32)],
    )


def per_device(
    count,
    points,
    tree_order,
    leaf_basis,
    local_transfer,
    local_coupling,
    device_transfer,
    device_coupling,
    solution,
    residual,
    direction,
):
    routes = partners(count)
    other = []
    for level in range(LEVELS - 1):
        matrix = local_transfer[6] if level == 0 else device_transfer[0, level - 1]
        other.append(lax.ppermute(matrix, "leaf", routes[level]))
    kernels = make_kernels(points, tree_order)
    tall, mix, paths = compose(leaf_basis, local_transfer, local_coupling)
    apply = (kernels, tall, mix)
    base, near, payload = begin(residual, direction, *apply)
    down = descend(local_transfer, device_transfer, device_coupling)
    up = flip(local_transfer, device_transfer, other)
    image = direction
    scalars = jnp.ones((8, COLS), F32)
    for step in range(ITERATIONS):
        field = None
        for level in range(LEVELS - 1):
            got = lax.ppermute(payload, "leaf", routes[level])
            payload, field = climb(level, payload, got, up, down, field)
        got = lax.ppermute(payload, "leaf", routes[LEVELS - 1])
        sweep = (payload, got, down, field)
        leaves = (leaf_basis, paths, base, near)
        if step + 1 < ITERATIONS:
            residual, direction, image, base, near, payload, scalars = turn(
                step == 0, sweep, scalars, leaves, residual, direction, image, apply
            )
            solution = solution + scalars[2:3] * direction
        else:
            residual, kept, direction, solution, scalars, sums = end(
                sweep, scalars, leaves, residual, direction, image, solution, count // 2
            )
    chip = sums + lax.ppermute(sums[0:1], "leaf", routes[0])
    same_core = [list(range(core, count, 2)) for core in range(2)]
    parts = lax.all_to_all(chip, "leaf", 0, 0, axis_index_groups=same_core, tiled=True)
    direction = call(last_kernel, "last", (parts, kept, direction, scalars), [vector_shape])[0]
    return (solution, residual, direction)


def solution(mesh):
    placed = (
        P(None, "leaf"),
        P("leaf", None),
        P("leaf", None, None),
        P("leaf", None, None),
        P("leaf", None, None),
        P("leaf", None, None, None),
        P("leaf", None, None, None),
        P("leaf", None),
        P("leaf", None),
        P("leaf", None),
    )
    return jax.shard_map(
        functools.partial(per_device, mesh.shape["leaf"]),
        mesh=mesh,
        in_specs=placed,
        out_specs=(P("leaf", None), P("leaf", None), P("leaf", None)),
        check_vma=False,
    )
```

profile of v0, /device:TPU:1, one launch (start us, length us, event | category | flops | bytes accessed | tf_op | source)
XLA Modules:
  0.0 175.7 jit_solution(11308417983654908096)
XLA Ops:
  2.0 2.6 %collective-permute-start.2 = (bf16[256,256]{1,0:T(8,128)(2,1)S(1)}, bf16[256,256]{1,0:T(8,128)(2,1)S(1)}, u32[]{:S(2)}, u32[]{:S(2)}) collective-permute-start(bf16[256,256]{1,0:T(8,128)(2,1)S(1)} %get-tuple-element.142), channel_id=1, source_target_pairs={{0,2},{1,3},{2,0},{3,1},{4,6},{5,7},{6,4},{7,5},{8,10},{9,11},{10,... | collective-permute-start | bytes 393224 | tf_op jit(solution)/shard_map/ppermute | solution.py:450
  4.6 3.0 %collective-permute-start.3 = (bf16[256,256]{1,0:T(8,128)(2,1)S(1)}, bf16[256,256]{1,0:T(8,128)(2,1)S(1)}, u32[]{:S(2)}, u32[]{:S(2)}) collective-permute-start(bf16[256,256]{1,0:T(8,128)(2,1)S(1)} %get-tuple-element.141), channel_id=1, source_target_pairs={{0,4},{1,5},{2,6},{3,7},{4,0},{5,1},{6,2},{7,3},{8,12},{9,13},{10,... | collective-permute-start | bytes 393224 | tf_op jit(solution)/shard_map/ppermute | solution.py:450
  7.6 3.3 %collective-permute-start.4 = (bf16[256,256]{1,0:T(8,128)(2,1)S(1)}, bf16[256,256]{1,0:T(8,128)(2,1)S(1)}, u32[]{:S(2)}, u32[]{:S(2)}) collective-permute-start(bf16[256,256]{1,0:T(8,128)(2,1)S(1)} %get-tuple-element.140), channel_id=1, source_target_pairs={{0,12},{1,13},{2,14},{3,15},{4,8},{5,9},{6,10},{7,11},{8,4},{9,5},... | collective-permute-start | bytes 393224 | tf_op jit(solution)/shard_map/ppermute | solution.py:450
  18.6 2.4 %collective-permute-start.1 = (bf16[256,256]{1,0:T(8,128)(2,1)S(1)}, bf16[256,256]{1,0:T(8,128)(2,1)S(1)}, u32[]{:S(2)}, u32[]{:S(2)}) collective-permute-start(bf16[256,256]{1,0:T(8,128)(2,1)S(1)} %slice_bitcast_fusion.6), channel_id=1, source_target_pairs={{0,1},{1,0},{2,3},{3,2},{4,5},{5,4},{6,7},{7,6},{8,9},{9,8},{10,11... | collective-permute-start | bytes 393224 | tf_op jit(solution)/shard_map/ppermute | solution.py:450
  20.9 3.4 %leaf_kernels.1.kernel.rest_6_.rest_7_ = bf16[4,512,512]{2,1,0:T(8,128)(2,1)S(1)} custom-call(f32[28,2048]{1,0:T(8,128)S(1)} %copy-done.8, s32[1,2048]{1,0:T(1,128)S(1)} %copy-done.9), custom_call_target="tpu_custom_call" | custom-call | flops 1241513984 | bytes 4194304 | tf_op jit(solution)/shard_map/leaf_kernels/pallas_call | solution.py:137
  29.0 2.4 %collective-permute-done.8.got = bf16[272,128]{1,0:T(8,128)(2,1)S(1)} collective-permute-done((bf16[272,128]{1,0:T(8,128)(2,1)S(1)}, bf16[272,128]{1,0:T(8,128)(2,1)S(1)}, u32[]{:S(2)}, u32[]{:S(2)}) %collective-permute-start.8) | collective-permute-done | bytes 69664 | tf_op jit(solution)/shard_map/ppermute | solution.py:462
  33.2 3.6 %collective-permute-done.9.got = bf16[272,128]{1,0:T(8,128)(2,1)S(1)} collective-permute-done((bf16[272,128]{1,0:T(8,128)(2,1)S(1)}, bf16[272,128]{1,0:T(8,128)(2,1)S(1)}, u32[]{:S(2)}, u32[]{:S(2)}) %collective-permute-start.9) | collective-permute-done | bytes 69664 | tf_op jit(solution)/shard_map/ppermute | solution.py:462
  37.2 5.3 %collective-permute-done.10.got = bf16[272,128]{1,0:T(8,128)(2,1)S(1)} collective-permute-done((bf16[272,128]{1,0:T(8,128)(2,1)S(1)}, bf16[272,128]{1,0:T(8,128)(2,1)S(1)}, u32[]{:S(2)}, u32[]{:S(2)}) %collective-permute-start.10) | collective-permute-done | bytes 69664 | tf_op jit(solution)/shard_map/ppermute | solution.py:462
  43.2 2.9 %collective-permute-done.11.got = bf16[272,128]{1,0:T(8,128)(2,1)S(1)} collective-permute-done((bf16[272,128]{1,0:T(8,128)(2,1)S(1)}, bf16[272,128]{1,0:T(8,128)(2,1)S(1)}, u32[]{:S(2)}, u32[]{:S(2)}) %collective-permute-start.11) | collective-permute-done | bytes 69664 | tf_op jit(solution)/shard_map/ppermute | solution.py:462
  47.3 3.6 %collective-permute-done.12.got = bf16[272,128]{1,0:T(8,128)(2,1)S(1)} collective-permute-done((bf16[272,128]{1,0:T(8,128)(2,1)S(1)}, bf16[272,128]{1,0:T(8,128)(2,1)S(1)}, u32[]{:S(2)}, u32[]{:S(2)}) %collective-permute-start.12) | collective-permute-done | bytes 69664 | tf_op jit(solution)/shard_map/ppermute | solution.py:462
  51.4 3.0 %collective-permute-done.13.got = bf16[272,128]{1,0:T(8,128)(2,1)S(1)} collective-permute-done((bf16[272,128]{1,0:T(8,128)(2,1)S(1)}, bf16[272,128]{1,0:T(8,128)(2,1)S(1)}, u32[]{:S(2)}, u32[]{:S(2)}) %collective-permute-start.13) | collective-permute-done | bytes 69664 | tf_op jit(solution)/shard_map/ppermute | solution.py:462
  56.7 2.5 %collective-permute-done.14.got = bf16[272,128]{1,0:T(8,128)(2,1)S(1)} collective-permute-done((bf16[272,128]{1,0:T(8,128)(2,1)S(1)}, bf16[272,128]{1,0:T(8,128)(2,1)S(1)}, u32[]{:S(2)}, u32[]{:S(2)}) %collective-permute-start.14) | collective-permute-done | bytes 69664 | tf_op jit(solution)/shard_map/ppermute | solution.py:464
  59.2 2.8 %turn.2 = (f32[2048,128]{1,0:T(8,128)S(1)}, f32[2048,128]{1,0:T(8,128)S(1)}, f32[2048,128]{1,0:T(8,128)S(1)}, f32[1024,128]{1,0:T(8,128)S(1)}, bf16[272,128]{1,0:T(8,128)(2,1)S(1)}, /*index=5*/f32[8,128]{1,0:T(8,128)S(1)}) custom-call(bf16[272,128]{1,0:T(8,128)(2,1)S(1)} %get-tuple-element.85.own, bf16[272,128]{1,0:T(8,128)(2,1)S(1)} %collective-permute-done.14.got, ...), custom_call_target="tpu_custom_call" | custom-call | tf_op jit(solution)/shard_map/turn/pallas_call | solution.py:86
  62.0 8.6 %collective-permute-start.15 = (bf16[272,128]{1,0:T(8,128)(2,1)S(1)}, bf16[272,128]{1,0:T(8,128)(2,1)S(1)}, u32[]{:S(2)}, u32[]{:S(2)}) collective-permute-start(bf16[272,128]{1,0:T(8,128)(2,1)S(1)} %get-tuple-element.90.own), channel_id=1, source_target_pairs={{0,1},{1,0},{2,3},{3,2},{4,5},{5,4},{6,7},{7,6},{8,9},{9,8},{10,11... | collective-permute-start | bytes 208904 | tf_op jit(solution)/shard_map/ppermute | solution.py:462
  71.9 3.1 %collective-permute-done.16.got = bf16[272,128]{1,0:T(8,128)(2,1)S(1)} collective-permute-done((bf16[272,128]{1,0:T(8,128)(2,1)S(1)}, bf16[272,128]{1,0:T(8,128)(2,1)S(1)}, u32[]{:S(2)}, u32[]{:S(2)}) %collective-permute-start.16) | collective-permute-done | bytes 69664 | tf_op jit(solution)/shard_map/ppermute | solution.py:462
  75.9 4.1 %collective-permute-done.17.got = bf16[272,128]{1,0:T(8,128)(2,1)S(1)} collective-permute-done((bf16[272,128]{1,0:T(8,128)(2,1)S(1)}, bf16[272,128]{1,0:T(8,128)(2,1)S(1)}, u32[]{:S(2)}, u32[]{:S(2)}) %collective-permute-start.17) | collective-permute-done | bytes 69664 | tf_op jit(solution)/shard_map/ppermute | solution.py:462
  80.4 5.3 %collective-permute-done.18.got = bf16[272,128]{1,0:T(8,128)(2,1)S(1)} collective-permute-done((bf16[272,128]{1,0:T(8,128)(2,1)S(1)}, bf16[272,128]{1,0:T(8,128)(2,1)S(1)}, u32[]{:S(2)}, u32[]{:S(2)}) %collective-permute-start.18) | collective-permute-done | bytes 69664 | tf_op jit(solution)/shard_map/ppermute | solution.py:462
  86.0 3.1 %collective-permute-done.19.got = bf16[272,128]{1,0:T(8,128)(2,1)S(1)} collective-permute-done((bf16[272,128]{1,0:T(8,128)(2,1)S(1)}, bf16[272,128]{1,0:T(8,128)(2,1)S(1)}, u32[]{:S(2)}, u32[]{:S(2)}) %collective-permute-start.19) | collective-permute-done | bytes 69664 | tf_op jit(solution)/shard_map/ppermute | solution.py:462
  90.4 3.5 %collective-permute-done.20.got = bf16[272,128]{1,0:T(8,128)(2,1)S(1)} collective-permute-done((bf16[272,128]{1,0:T(8,128)(2,1)S(1)}, bf16[272,128]{1,0:T(8,128)(2,1)S(1)}, u32[]{:S(2)}, u32[]{:S(2)}) %collective-permute-start.20) | collective-permute-done | bytes 69664 | tf_op jit(solution)/shard_map/ppermute | solution.py:462
  94.3 3.1 %collective-permute-done.21.got = bf16[272,128]{1,0:T(8,128)(2,1)S(1)} collective-permute-done((bf16[272,128]{1,0:T(8,128)(2,1)S(1)}, bf16[272,128]{1,0:T(8,128)(2,1)S(1)}, u32[]{:S(2)}, u32[]{:S(2)}) %collective-permute-start.21) | collective-permute-done | bytes 69664 | tf_op jit(solution)/shard_map/ppermute | solution.py:462
  100.0 2.5 %collective-permute-done.22.got = bf16[272,128]{1,0:T(8,128)(2,1)S(1)} collective-permute-done((bf16[272,128]{1,0:T(8,128)(2,1)S(1)}, bf16[272,128]{1,0:T(8,128)(2,1)S(1)}, u32[]{:S(2)}, u32[]{:S(2)}) %collective-permute-start.22) | collective-permute-done | bytes 69664 | tf_op jit(solution)/shard_map/ppermute | solution.py:464
  102.4 2.8 %turn.3 = (f32[2048,128]{1,0:T(8,128)S(1)}, f32[2048,128]{1,0:T(8,128)S(1)}, f32[2048,128]{1,0:T(8,128)S(1)}, f32[2048,128]{1,0:T(8,128)S(1)}, f32[1024,128]{1,0...) custom-call(bf16[272,128]{1,0:T(8,128)(2,1)S(1)} %get-tuple-element.103.own, ...), custom_call_target="tpu_custom_call" | custom-call | tf_op jit(solution)/shard_map/turn/pallas_call | solution.py:86
  105.3 8.5 %collective-permute-start.23 = (bf16[272,128]{1,0:T(8,128)(2,1)S(1)}, bf16[272,128]{1,0:T(8,128)(2,1)S(1)}, u32[]{:S(2)}, u32[]{:S(2)}) collective-permute-start(bf16[272,128]{1,0:T(8,128)(2,1)S(1)} %get-tuple-element.110.own), channel_id=1, source_target_pairs={{0,1},{1,0},{2,3},{3,2},{4,5},{5,4},{6,7},{7,6},{8,9},{9,8},{10,11... | collective-permute-start | bytes 208904 | tf_op jit(solution)/shard_map/ppermute | solution.py:462
  115.0 3.1 %collective-permute-done.24.got = bf16[272,128]{1,0:T(8,128)(2,1)S(1)} collective-permute-done((bf16[272,128]{1,0:T(8,128)(2,1)S(1)}, bf16[272,128]{1,0:T(8,128)(2,1)S(1)}, u32[]{:S(2)}, u32[]{:S(2)}) %collective-permute-start.24) | collective-permute-done | bytes 69664 | tf_op jit(solution)/shard_map/ppermute | solution.py:462
  119.7 3.7 %collective-permute-done.25.got = bf16[272,128]{1,0:T(8,128)(2,1)S(1)} collective-permute-done((bf16[272,128]{1,0:T(8,128)(2,1)S(1)}, bf16[272,128]{1,0:T(8,128)(2,1)S(1)}, u32[]{:S(2)}, u32[]{:S(2)}) %collective-permute-start.25) | collective-permute-done | bytes 69664 | tf_op jit(solution)/shard_map/ppermute | solution.py:462
  123.8 5.3 %collective-permute-done.26.got = bf16[272,128]{1,0:T(8,128)(2,1)S(1)} collective-permute-done((bf16[272,128]{1,0:T(8,128)(2,1)S(1)}, bf16[272,128]{1,0:T(8,128)(2,1)S(1)}, u32[]{:S(2)}, u32[]{:S(2)}) %collective-permute-start.26) | collective-permute-done | bytes 69664 | tf_op jit(solution)/shard_map/ppermute | solution.py:462
  129.4 3.1 %collective-permute-done.27.got = bf16[272,128]{1,0:T(8,128)(2,1)S(1)} collective-permute-done((bf16[272,128]{1,0:T(8,128)(2,1)S(1)}, bf16[272,128]{1,0:T(8,128)(2,1)S(1)}, u32[]{:S(2)}, u32[]{:S(2)}) %collective-permute-start.27) | collective-permute-done | bytes 69664 | tf_op jit(solution)/shard_map/ppermute | solution.py:462
  133.8 3.5 %collective-permute-done.28.got = bf16[272,128]{1,0:T(8,128)(2,1)S(1)} collective-permute-done((bf16[272,128]{1,0:T(8,128)(2,1)S(1)}, bf16[272,128]{1,0:T(8,128)(2,1)S(1)}, u32[]{:S(2)}, u32[]{:S(2)}) %collective-permute-start.28) | collective-permute-done | bytes 69664 | tf_op jit(solution)/shard_map/ppermute | solution.py:462
  137.8 3.1 %collective-permute-done.29.got = bf16[272,128]{1,0:T(8,128)(2,1)S(1)} collective-permute-done((bf16[272,128]{1,0:T(8,128)(2,1)S(1)}, bf16[272,128]{1,0:T(8,128)(2,1)S(1)}, u32[]{:S(2)}, u32[]{:S(2)}) %collective-permute-start.29) | collective-permute-done | bytes 69664 | tf_op jit(solution)/shard_map/ppermute | solution.py:462
  143.3 2.3 %collective-permute-done.30.got = bf16[272,128]{1,0:T(8,128)(2,1)S(1)} collective-permute-done((bf16[272,128]{1,0:T(8,128)(2,1)S(1)}, bf16[272,128]{1,0:T(8,128)(2,1)S(1)}, u32[]{:S(2)}, u32[]{:S(2)}) %collective-permute-start.30) | collective-permute-done | bytes 69664 | tf_op jit(solution)/shard_map/ppermute | solution.py:464
  147.9 8.0 %collective-permute-start.31 = (f32[1,128]{1,0:T(1,128)S(1)}, f32[1,128]{1,0:T(1,128)S(1)}, u32[]{:S(2)}, u32[]{:S(2)}) collective-permute-start(f32[1,128]{1,0:T(1,128)S(1)} %slice.39), channel_id=1, source_target_pairs={{0,1},{1,0},{2,3},{3,2},{4,5},{5,4},{6,7},{7,6},{8,9},{9,8},{10,11... | collective-permute-start | bytes 1544 | tf_op jit(solution)/shard_map/ppermute | solution.py:476
  156.8 17.8 %all_to_all.11 = f32[128,1,128]{2,1,0:T(1,128)S(1)} all-to-all(f32[128,1,128]{2,1,0:T(1,128)S(1)} %bitcast.24), channel_id=1, replica_groups={{0,2,4,6,8,10,12,14,16,18,20,22,24,26,28,30,32,34,36,38,40,42,44,46,48,..., dimensions={0} | all-to-all | bytes 131072 | tf_op jit(solution)/shard_map/all_to_all | solution.py:478
  (93 shorter events, 39.2 us)
Async XLA Ops:
  2.0 15.1 %collective-permute-start.2 = (bf16[256,256]{1,0:T(8,128)(2,1)S(1)}, bf16[256,256]{1,0:T(8,128)(2,1)S(1)}, u32[]{:S(2)}, u32[]{:S(2)}) collective-permute-start(bf16[256,256]{1,0:T(8,128)(2,1)S(1)} %get-tuple-element.142), channel_id=1, source_target_pairs={{0,2},{1,3},{2,0},{3,1},{4,6},{5,7},{6,4},{7,5},{8,10},{9,11},{10,... | collective-permute-start | bytes 393224 | tf_op jit(solution)/shard_map/ppermute | solution.py:450
  4.6 14.0 %collective-permute-start.3 = (bf16[256,256]{1,0:T(8,128)(2,1)S(1)}, bf16[256,256]{1,0:T(8,128)(2,1)S(1)}, u32[]{:S(2)}, u32[]{:S(2)}) collective-permute-start(bf16[256,256]{1,0:T(8,128)(2,1)S(1)} %get-tuple-element.141), channel_id=1, source_target_pairs={{0,4},{1,5},{2,6},{3,7},{4,0},{5,1},{6,2},{7,3},{8,12},{9,13},{10,... | collective-permute-start | bytes 393224 | tf_op jit(solution)/shard_map/ppermute | solution.py:450
  7.6 18.6 %collective-permute-start.4 = (bf16[256,256]{1,0:T(8,128)(2,1)S(1)}, bf16[256,256]{1,0:T(8,128)(2,1)S(1)}, u32[]{:S(2)}, u32[]{:S(2)}) collective-permute-start(bf16[256,256]{1,0:T(8,128)(2,1)S(1)} %get-tuple-element.140), channel_id=1, source_target_pairs={{0,12},{1,13},{2,14},{3,15},{4,8},{5,9},{6,10},{7,11},{8,4},{9,5},... | collective-permute-start | bytes 393224 | tf_op jit(solution)/shard_map/ppermute | solution.py:450
  10.9 16.4 %collective-permute-start.5 = (bf16[256,256]{1,0:T(8,128)(2,1)S(1)}, bf16[256,256]{1,0:T(8,128)(2,1)S(1)}, u32[]{:S(2)}, u32[]{:S(2)}) collective-permute-start(bf16[256,256]{1,0:T(8,128)(2,1)S(1)} %get-tuple-element.139), channel_id=1, source_target_pairs={{0,16},{1,17},{2,18},{3,19},{4,20},{5,21},{6,22},{7,23},{8,24},{9,... | collective-permute-start | bytes 393224 | tf_op jit(solution)/shard_map/ppermute | solution.py:450
  12.1 15.2 %collective-permute-start.6 = (bf16[256,256]{1,0:T(8,128)(2,1)S(1)}, bf16[256,256]{1,0:T(8,128)(2,1)S(1)}, u32[]{:S(2)}, u32[]{:S(2)}) collective-permute-start(bf16[256,256]{1,0:T(8,128)(2,1)S(1)} %get-tuple-element.138), channel_id=1, source_target_pairs={{0,48},{1,49},{2,50},{3,51},{4,52},{5,53},{6,54},{7,55},{8,56},{9,... | collective-permute-start | bytes 393224 | tf_op jit(solution)/shard_map/ppermute | solution.py:450
  17.2 10.2 %collective-permute-start.7 = (bf16[256,256]{1,0:T(8,128)(2,1)S(1)}, bf16[256,256]{1,0:T(8,128)(2,1)S(1)}, u32[]{:S(2)}, u32[]{:S(2)}) collective-permute-start(bf16[256,256]{1,0:T(8,128)(2,1)S(1)} %get-tuple-element.137), channel_id=1, source_target_pairs={{0,64},{1,65},{2,66},{3,67},{4,68},{5,69},{6,70},{7,71},{8,72},{9,... | collective-permute-start | bytes 393224 | tf_op jit(solution)/shard_map/ppermute | solution.py:450
  18.6 8.8 %collective-permute-start.1 = (bf16[256,256]{1,0:T(8,128)(2,1)S(1)}, bf16[256,256]{1,0:T(8,128)(2,1)S(1)}, u32[]{:S(2)}, u32[]{:S(2)}) collective-permute-start(bf16[256,256]{1,0:T(8,128)(2,1)S(1)} %slice_bitcast_fusion.6), channel_id=1, source_target_pairs={{0,1},{1,0},{2,3},{3,2},{4,5},{5,4},{6,7},{7,6},{8,9},{9,8},{10,11... | collective-permute-start | bytes 393224 | tf_op jit(solution)/shard_map/ppermute | solution.py:450
  26.2 1.7 collective-permute-start
  28.2 3.2 %collective-permute-start.8 = (bf16[272,128]{1,0:T(8,128)(2,1)S(1)}, bf16[272,128]{1,0:T(8,128)(2,1)S(1)}, u32[]{:S(2)}, u32[]{:S(2)}) collective-permute-start(bf16[272,128]{1,0:T(8,128)(2,1)S(1)} %get-tuple-element.73.own), channel_id=1, source_target_pairs={{0,2},{1,3},{2,0},{3,1},{4,6},{5,7},{6,4},{7,5},{8,10},{9,11},{10,... | collective-permute-start | bytes 208904 | tf_op jit(solution)/shard_map/ppermute | solution.py:462
  31.7 5.1 %collective-permute-start.9 = (bf16[272,128]{1,0:T(8,128)(2,1)S(1)}, bf16[272,128]{1,0:T(8,128)(2,1)S(1)}, u32[]{:S(2)}, u32[]{:S(2)}) collective-permute-start(bf16[272,128]{1,0:T(8,128)(2,1)S(1)} %get-tuple-element.75.own), channel_id=1, source_target_pairs={{0,4},{1,5},{2,6},{3,7},{4,0},{5,1},{6,2},{7,3},{8,12},{9,13},{10,... | collective-permute-start | bytes 208904 | tf_op jit(solution)/shard_map/ppermute | solution.py:462
  37.1 5.4 %collective-permute-start.10 = (bf16[272,128]{1,0:T(8,128)(2,1)S(1)}, bf16[272,128]{1,0:T(8,128)(2,1)S(1)}, u32[]{:S(2)}, u32[]{:S(2)}) collective-permute-start(bf16[272,128]{1,0:T(8,128)(2,1)S(1)} %get-tuple-element.77.own), channel_id=1, source_target_pairs={{0,12},{1,13},{2,14},{3,15},{4,8},{5,9},{6,10},{7,11},{8,4},{9,5},... | collective-permute-start | bytes 208904 | tf_op jit(solution)/shard_map/ppermute | solution.py:462
  42.8 3.3 %collective-permute-start.11 = (bf16[272,128]{1,0:T(8,128)(2,1)S(1)}, bf16[272,128]{1,0:T(8,128)(2,1)S(1)}, u32[]{:S(2)}, u32[]{:S(2)}) collective-permute-start(bf16[272,128]{1,0:T(8,128)(2,1)S(1)} %get-tuple-element.79.own), channel_id=1, source_target_pairs={{0,16},{1,17},{2,18},{3,19},{4,20},{5,21},{6,22},{7,23},{8,24},{9,... | collective-permute-start | bytes 208904 | tf_op jit(solution)/shard_map/ppermute | solution.py:462
  46.4 4.5 %collective-permute-start.12 = (bf16[272,128]{1,0:T(8,128)(2,1)S(1)}, bf16[272,128]{1,0:T(8,128)(2,1)S(1)}, u32[]{:S(2)}, u32[]{:S(2)}) collective-permute-start(bf16[272,128]{1,0:T(8,128)(2,1)S(1)} %get-tuple-element.81.own), channel_id=1, source_target_pairs={{0,48},{1,49},{2,50},{3,51},{4,52},{5,53},{6,54},{7,55},{8,56},{9,... | collective-permute-start | bytes 208904 | tf_op jit(solution)/shard_map/ppermute | solution.py:462
  51.2 3.2 %collective-permute-start.13 = (bf16[272,128]{1,0:T(8,128)(2,1)S(1)}, bf16[272,128]{1,0:T(8,128)(2,1)S(1)}, u32[]{:S(2)}, u32[]{:S(2)}) collective-permute-start(bf16[272,128]{1,0:T(8,128)(2,1)S(1)} %get-tuple-element.83.own), channel_id=1, source_target_pairs={{0,64},{1,65},{2,66},{3,67},{4,68},{5,69},{6,70},{7,71},{8,72},{9,... | collective-permute-start | bytes 208904 | tf_op jit(solution)/shard_map/ppermute | solution.py:462
  54.7 4.5 %collective-permute-start.14 = (bf16[272,128]{1,0:T(8,128)(2,1)S(1)}, bf16[272,128]{1,0:T(8,128)(2,1)S(1)}, u32[]{:S(2)}, u32[]{:S(2)}) collective-permute-start(bf16[272,128]{1,0:T(8,128)(2,1)S(1)} %get-tuple-element.85.own), channel_id=1, source_target_pairs={{0,192},{1,193},{2,194},{3,195},{4,196},{5,197},{6,198},{7,199},{8... | collective-permute-start | bytes 208904 | tf_op jit(solution)/shard_map/ppermute | solution.py:464
  62.0 9.5 %collective-permute-start.15 = (bf16[272,128]{1,0:T(8,128)(2,1)S(1)}, bf16[272,128]{1,0:T(8,128)(2,1)S(1)}, u32[]{:S(2)}, u32[]{:S(2)}) collective-permute-start(bf16[272,128]{1,0:T(8,128)(2,1)S(1)} %get-tuple-element.90.own), channel_id=1, source_target_pairs={{0,1},{1,0},{2,3},{3,2},{4,5},{5,4},{6,7},{7,6},{8,9},{9,8},{10,11... | collective-permute-start | bytes 208904 | tf_op jit(solution)/shard_map/ppermute | solution.py:462
  71.8 3.2 %collective-permute-start.16 = (bf16[272,128]{1,0:T(8,128)(2,1)S(1)}, bf16[272,128]{1,0:T(8,128)(2,1)S(1)}, u32[]{:S(2)}, u32[]{:S(2)}) collective-permute-start(bf16[272,128]{1,0:T(8,128)(2,1)S(1)} %get-tuple-element.91.own), channel_id=1, source_target_pairs={{0,2},{1,3},{2,0},{3,1},{4,6},{5,7},{6,4},{7,5},{8,10},{9,11},{10,... | collective-permute-start | bytes 208904 | tf_op jit(solution)/shard_map/ppermute | solution.py:462
  75.3 4.6 %collective-permute-start.17 = (bf16[272,128]{1,0:T(8,128)(2,1)S(1)}, bf16[272,128]{1,0:T(8,128)(2,1)S(1)}, u32[]{:S(2)}, u32[]{:S(2)}) collective-permute-start(bf16[272,128]{1,0:T(8,128)(2,1)S(1)} %get-tuple-element.93.own), channel_id=1, source_target_pairs={{0,4},{1,5},{2,6},{3,7},{4,0},{5,1},{6,2},{7,3},{8,12},{9,13},{10,... | collective-permute-start | bytes 208904 | tf_op jit(solution)/shard_map/ppermute | solution.py:462
  80.3 5.4 %collective-permute-start.18 = (bf16[272,128]{1,0:T(8,128)(2,1)S(1)}, bf16[272,128]{1,0:T(8,128)(2,1)S(1)}, u32[]{:S(2)}, u32[]{:S(2)}) collective-permute-start(bf16[272,128]{1,0:T(8,128)(2,1)S(1)} %get-tuple-element.95.own), channel_id=1, source_target_pairs={{0,12},{1,13},{2,14},{3,15},{4,8},{5,9},{6,10},{7,11},{8,4},{9,5},... | collective-permute-start | bytes 208904 | tf_op jit(solution)/shard_map/ppermute | solution.py:462
  85.9 3.2 %collective-permute-start.19 = (bf16[272,128]{1,0:T(8,128)(2,1)S(1)}, bf16[272,128]{1,0:T(8,128)(2,1)S(1)}, u32[]{:S(2)}, u32[]{:S(2)}) collective-permute-start(bf16[272,128]{1,0:T(8,128)(2,1)S(1)} %get-tuple-element.97.own), channel_id=1, source_target_pairs={{0,16},{1,17},{2,18},{3,19},{4,20},{5,21},{6,22},{7,23},{8,24},{9,... | collective-permute-start | bytes 208904 | tf_op jit(solution)/shard_map/ppermute | solution.py:462
  89.5 4.5 %collective-permute-start.20 = (bf16[272,128]{1,0:T(8,128)(2,1)S(1)}, bf16[272,128]{1,0:T(8,128)(2,1)S(1)}, u32[]{:S(2)}, u32[]{:S(2)}) collective-permute-start(bf16[272,128]{1,0:T(8,128)(2,1)S(1)} %get-tuple-element.99.own), channel_id=1, source_target_pairs={{0,48},{1,49},{2,50},{3,51},{4,52},{5,53},{6,54},{7,55},{8,56},{9,... | collective-permute-start | bytes 208904 | tf_op jit(solution)/shard_map/ppermute | solution.py:462
  94.2 3.2 %collective-permute-start.21 = (bf16[272,128]{1,0:T(8,128)(2,1)S(1)}, bf16[272,128]{1,0:T(8,128)(2,1)S(1)}, u32[]{:S(2)}, u32[]{:S(2)}) collective-permute-start(bf16[272,128]{1,0:T(8,128)(2,1)S(1)} %get-tuple-element.101.own), channel_id=1, source_target_pairs={{0,64},{1,65},{2,66},{3,67},{4,68},{5,69},{6,70},{7,71},{8,72},{9,... | collective-permute-start | bytes 208904 | tf_op jit(solution)/shard_map/ppermute | solution.py:462
  97.8 4.7 %collective-permute-start.22 = (bf16[272,128]{1,0:T(8,128)(2,1)S(1)}, bf16[272,128]{1,0:T(8,128)(2,1)S(1)}, u32[]{:S(2)}, u32[]{:S(2)}) collective-permute-start(bf16[272,128]{1,0:T(8,128)(2,1)S(1)} %get-tuple-element.103.own), channel_id=1, source_target_pairs={{0,192},{1,193},{2,194},{3,195},{4,196},{5,197},{6,198},{7,199},{8... | collective-permute-start | bytes 208904 | tf_op jit(solution)/shard_map/ppermute | solution.py:464
  105.3 9.4 %collective-permute-start.23 = (bf16[272,128]{1,0:T(8,128)(2,1)S(1)}, bf16[272,128]{1,0:T(8,128)(2,1)S(1)}, u32[]{:S(2)}, u32[]{:S(2)}) collective-permute-start(bf16[272,128]{1,0:T(8,128)(2,1)S(1)} %get-tuple-element.110.own), channel_id=1, source_target_pairs={{0,1},{1,0},{2,3},{3,2},{4,5},{5,4},{6,7},{7,6},{8,9},{9,8},{10,11... | collective-permute-start | bytes 208904 | tf_op jit(solution)/shard_map/ppermute | solution.py:462
  114.9 3.2 %collective-permute-start.24 = (bf16[272,128]{1,0:T(8,128)(2,1)S(1)}, bf16[272,128]{1,0:T(8,128)(2,1)S(1)}, u32[]{:S(2)}, u32[]{:S(2)}) collective-permute-start(bf16[272,128]{1,0:T(8,128)(2,1)S(1)} %get-tuple-element.111.own), channel_id=1, source_target_pairs={{0,2},{1,3},{2,0},{3,1},{4,6},{5,7},{6,4},{7,5},{8,10},{9,11},{10,... | collective-permute-start | bytes 208904 | tf_op jit(solution)/shard_map/ppermute | solution.py:462
  118.5 4.9 %collective-permute-start.25 = (bf16[272,128]{1,0:T(8,128)(2,1)S(1)}, bf16[272,128]{1,0:T(8,128)(2,1)S(1)}, u32[]{:S(2)}, u32[]{:S(2)}) collective-permute-start(bf16[272,128]{1,0:T(8,128)(2,1)S(1)} %get-tuple-element.113.own), channel_id=1, source_target_pairs={{0,4},{1,5},{2,6},{3,7},{4,0},{5,1},{6,2},{7,3},{8,12},{9,13},{10,... | collective-permute-start | bytes 208904 | tf_op jit(solution)/shard_map/ppermute | solution.py:462
  123.7 5.4 %collective-permute-start.26 = (bf16[272,128]{1,0:T(8,128)(2,1)S(1)}, bf16[272,128]{1,0:T(8,128)(2,1)S(1)}, u32[]{:S(2)}, u32[]{:S(2)}) collective-permute-start(bf16[272,128]{1,0:T(8,128)(2,1)S(1)} %get-tuple-element.115.own), channel_id=1, source_target_pairs={{0,12},{1,13},{2,14},{3,15},{4,8},{5,9},{6,10},{7,11},{8,4},{9,5},... | collective-permute-start | bytes 208904 | tf_op jit(solution)/shard_map/ppermute | solution.py:462
  129.3 3.2 %collective-permute-start.27 = (bf16[272,128]{1,0:T(8,128)(2,1)S(1)}, bf16[272,128]{1,0:T(8,128)(2,1)S(1)}, u32[]{:S(2)}, u32[]{:S(2)}) collective-permute-start(bf16[272,128]{1,0:T(8,128)(2,1)S(1)} %get-tuple-element.117.own), channel_id=1, source_target_pairs={{0,16},{1,17},{2,18},{3,19},{4,20},{5,21},{6,22},{7,23},{8,24},{9,... | collective-permute-start | bytes 208904 | tf_op jit(solution)/shard_map/ppermute | solution.py:462
  132.9 4.5 %collective-permute-start.28 = (bf16[272,128]{1,0:T(8,128)(2,1)S(1)}, bf16[272,128]{1,0:T(8,128)(2,1)S(1)}, u32[]{:S(2)}, u32[]{:S(2)}) collective-permute-start(bf16[272,128]{1,0:T(8,128)(2,1)S(1)} %get-tuple-element.119.own), channel_id=1, source_target_pairs={{0,48},{1,49},{2,50},{3,51},{4,52},{5,53},{6,54},{7,55},{8,56},{9,... | collective-permute-start | bytes 208904 | tf_op jit(solution)/shard_map/ppermute | solution.py:462
  137.7 3.2 %collective-permute-start.29 = (bf16[272,128]{1,0:T(8,128)(2,1)S(1)}, bf16[272,128]{1,0:T(8,128)(2,1)S(1)}, u32[]{:S(2)}, u32[]{:S(2)}) collective-permute-start(bf16[272,128]{1,0:T(8,128)(2,1)S(1)} %get-tuple-element.121.own), channel_id=1, source_target_pairs={{0,64},{1,65},{2,66},{3,67},{4,68},{5,69},{6,70},{7,71},{8,72},{9,... | collective-permute-start | bytes 208904 | tf_op jit(solution)/shard_map/ppermute | solution.py:462
  141.2 4.5 %collective-permute-start.30 = (bf16[272,128]{1,0:T(8,128)(2,1)S(1)}, bf16[272,128]{1,0:T(8,128)(2,1)S(1)}, u32[]{:S(2)}, u32[]{:S(2)}) collective-permute-start(bf16[272,128]{1,0:T(8,128)(2,1)S(1)} %get-tuple-element.123.own), channel_id=1, source_target_pairs={{0,192},{1,193},{2,194},{3,195},{4,196},{5,197},{6,198},{7,199},{8... | collective-permute-start | bytes 208904 | tf_op jit(solution)/shard_map/ppermute | solution.py:464
  147.9 8.9 %collective-permute-start.31 = (f32[1,128]{1,0:T(1,128)S(1)}, f32[1,128]{1,0:T(1,128)S(1)}, u32[]{:S(2)}, u32[]{:S(2)}) collective-permute-start(f32[1,128]{1,0:T(1,128)S(1)} %slice.39), channel_id=1, source_target_pairs={{0,1},{1,0},{2,3},{3,2},{4,5},{5,4},{6,7},{7,6},{8,9},{9,8},{10,11... | collective-permute-start | bytes 1544 | tf_op jit(solution)/shard_map/ppermute | solution.py:476
  (11 other events, 92.6 us)
where the time goes:
time: 176 us
  waiting for transfers between devices  74.9 us (43%)
  starting transfers between devices  55.3 us (31%)
  Pallas kernels  23 us (13%)
  blocking collectives  17.8 us (10%)
  local copies, waits for them, and re-layouts  3.52 us (2%)
    ppermute x21, waiting for transfers between devices, per_device(): got = lax.ppermute(payload, 'leaf', routes[level])  66.8 us
    ppermute x21, starting transfers between devices, per_device(): got = lax.ppermute(payload, 'leaf', routes[level])  25.4 us
    all_to_all x1, blocking collectives, per_device(): lax.all_to_all(chip, 'leaf', 0, 0, axis_index_groups=same_core, tiled=True)  17.8 us
    ppermute x7, starting transfers between devices, per_device(): other.append(lax.ppermute(matrix, 'leaf', routes[level]))  15.6 us
    pallas_call x7, Pallas kernels, call(): pl.pallas_call(kernel, in_specs=[in_vmem] * len(operands), out_specs=[in_...  12.8 us
    ppermute x1, starting transfers between devices, per_device(): chip = sums + lax.ppermute(sums[0:1], 'leaf', routes[0])  8.05 us
    ppermute x3, waiting for transfers between devices, per_device(): got = lax.ppermute(payload, 'leaf', routes[LEVELS - 1])  7.25 us
    pallas_call x21, Pallas kernels, climb(): pl.pallas_call(functools.partial(climb_kernel, level), in_specs=[in_vmem]...  6.28 us
  transfers between devices with their start and end apart: 32, of which 24 were waited for; matrix products, arithmetic and copies ran while one was open for 1% of the time, Pallas kernels for 4%

commit v1 on v0

--- a/solution.py
+++ b/solution.py
@@ -149,7 +149,10 @@
     )(points, order)
 
 
-def compose_kernel(basis, local_r, local_b, tall, mix, paths):
+def compose_kernel(basis, local_r, local_b, device_r, _, tall, mix, paths, *steps):
+    for level in range(LEVELS - 1):
+        step = local_r[LEAVES + 2] if level == 0 else device_r[0, level - 1]
+        steps[level][...] = step.T
     first = [local_r[i] for i in range(LEAVES)]
     second = [local_r[LEAVES], local_r[LEAVES + 1]]
     flipped = [block.T for block in first]
@@ -174,18 +177,20 @@
             mix[i * RANK : (i + 1) * RANK, j * RANK : (j + 1) * RANK] = block
 
 
-def compose(basis, local_r, local_b):
+def compose(basis, local_r, local_b, device_r, after):
     shapes = [
         (LEAVES, RANK, ROWS),
         ((LEAVES + 1) * RANK, LEAVES * RANK),
         (LEAVES * RANK, RANK),
-    ]
-    return call(
+    ] + [(RANK, RANK)] * (LEVELS - 1)
+    return pl.pallas_call(
         compose_kernel,
-        "compose",
-        (basis, local_r, local_b),
-        [jax.ShapeDtypeStruct(shape, BF) for shape in shapes],
-    )
+        in_specs=[in_vmem] * 4 + [pl.BlockSpec(memory_space=pl.ANY)],
+        out_specs=[in_vmem] * len(shapes),
+        out_shape=[jax.ShapeDtypeStruct(shape, BF) for shape in shapes],
+        compiler_params=params(),
+        name="compose",
+    )(basis, local_r, local_b, device_r, after)
 
 
 def descend_kernel(local_r, device_r, device_b, down):
@@ -211,31 +216,12 @@
     )[0]
 
 
-def flip_kernel(local_r, device_r, *rest):
-    out = rest[-1]
-    for level in range(LEVELS - 1):
-        step = local_r[LEAVES + 2] if level == 0 else device_r[0, level - 1]
-        out[level, :, :RANK] = step.T
-        out[level, :, RANK:] = rest[level][...].T
-
-
-def flip(local_r, device_r, other_r):
-    return pl.pallas_call(
-        flip_kernel,
-        in_specs=[in_vmem] * (2 + len(other_r)),
-        out_specs=in_vmem,
-        out_shape=jax.ShapeDtypeStruct((LEVELS - 1, RANK, 2 * RANK), BF),
-        compiler_params=params(),
-        name="flip",
-    )(local_r, device_r, *other_r)
-
-
-def climb_kernel(level, own, got, up, down, *rest):
+def climb_kernel(level, own, got, step, other, down, *rest):
     field_in = rest[0] if level else None
     out, field_out = rest[-2:]
     mine = own[:RANK]
     theirs = got[:RANK]
-    out[:RANK] = dot(up[level], jnp.concatenate([mine, theirs], axis=0)).astype(BF)
+    out[:RANK] = (dot(step[...], mine) + dot(other[...], theirs)).astype(BF)
     felt = dot(down[level], theirs)
     energy = jnp.sum(mine.astype(F32) * felt[:RANK], axis=0, keepdims=True)
     zero = jnp.zeros_like(energy)
@@ -247,8 +233,8 @@
         field_out[...] = felt[RANK:]
 
 
-def climb(level, own, got, up, down, field):
-    operands = [own, got, up, down] + ([field] if level else [])
+def climb(level, own, got, step, other, down, field):
+    operands = [own, got, step, other, down] + ([field] if level else [])
     return pl.pallas_call(
         functools.partial(climb_kernel, level),
         in_specs=[in_vmem] * len(operands),
@@ -444,23 +430,23 @@
     direction,
 ):
     routes = partners(count)
-    other = []
-    for level in range(LEVELS - 1):
-        matrix = local_transfer[6] if level == 0 else device_transfer[0, level - 1]
-        other.append(lax.ppermute(matrix, "leaf", routes[level]))
     kernels = make_kernels(points, tree_order)
-    tall, mix, paths = compose(leaf_basis, local_transfer, local_coupling)
+    tall, mix, paths, *steps = compose(
+        leaf_basis, local_transfer, local_coupling, device_transfer, kernels
+    )
+    others = [lax.ppermute(block, "leaf", route) for block, route in zip(steps, routes)]
     apply = (kernels, tall, mix)
     base, near, payload = begin(residual, direction, *apply)
     down = descend(local_transfer, device_transfer, device_coupling)
-    up = flip(local_transfer, device_transfer, other)
     image = direction
     scalars = jnp.ones((8, COLS), F32)
     for step in range(ITERATIONS):
         field = None
         for level in range(LEVELS - 1):
             got = lax.ppermute(payload, "leaf", routes[level])
-            payload, field = climb(level, payload, got, up, down, field)
+            payload, field = climb(
+                level, payload, got, steps[level], others[level], down, field
+            )
         got = lax.ppermute(payload, "leaf", routes[LEVELS - 1])
         sweep = (payload, got, down, field)
         leaves = (leaf_basis, paths, base, near)

time: 176 us -> 170 us (0.966)
  waiting for transfers between devices: 74.9 us -> 51.9 us
  starting transfers between devices: 55.3 us -> 69.5 us
  blocking collectives: 17.8 us -> 23.3 us
    ppermute x21, waiting for transfers between devices: 66.8 us -> 45.2 us  [per_device(): got = lax.ppermute(payload, 'leaf', routes[level])]
    ppermute x21, starting transfers between devices: 25.4 us -> 41 us  [per_device(): got = lax.ppermute(payload, 'leaf', routes[level])]
    all_to_all x1, blocking collectives: 17.8 us -> 23.3 us  [per_device(): lax.all_to_all(chip, 'leaf', 0, 0, axis_index_groups=same_core, tiled=True)]
    squeeze x2 -> x0, local copies, waits for them, and re-layouts: 2.28 us -> none  [per_device(): matrix = local_transfer[6] if level == 0 else device_transfer[0, level - 1]]
    ppermute x7, starting transfers between devices: 15.6 us -> 13.6 us  [per_device(): lax.ppermute(block, 'leaf', route)]
    ppermute x3, waiting for transfers between devices: 7.25 us -> 5.32 us  [per_device(): got = lax.ppermute(payload, 'leaf', routes[LEVELS - 1])]
    ppermute x3, starting transfers between devices: 6.19 us -> 8.04 us  [per_device(): got = lax.ppermute(payload, 'leaf', routes[LEVELS - 1])]
    pallas_call x7 -> x6, Pallas kernels: 12.8 us -> 11.7 us  [call(): pl.pallas_call(kernel, in_specs=[in_vmem] * len(operands), out_specs=[in_...]
  transfers between devices with their start and end apart: 32 -> 32, of which waited for: 24 -> 25; matrix products, arithmetic and copies ran while one was open for 1% -> 0% of each run, Pallas kernels for 4% -> 3%
where the time goes in v1:
time: 170 us
  starting transfers between devices  69.5 us (41%)
  waiting for transfers between devices  51.9 us (31%)
  blocking collectives  23.3 us (14%)
  Pallas kernels  22.6 us (13%)
  local copies, waits for them, and re-layouts  1.84 us (1%)
    ppermute x21, waiting for transfers between devices, per_device(): got = lax.ppermute(payload, 'leaf', routes[level])  45.2 us
    ppermute x21, starting transfers between devices, per_device(): got = lax.ppermute(payload, 'leaf', routes[level])  41 us
    all_to_all x1, blocking collectives, per_device(): lax.all_to_all(chip, 'leaf', 0, 0, axis_index_groups=same_core, tiled=True)  23.3 us
    ppermute x7, starting transfers between devices, per_device(): lax.ppermute(block, 'leaf', route)  13.6 us
    pallas_call x6, Pallas kernels, call(): pl.pallas_call(kernel, in_specs=[in_vmem] * len(operands), out_specs=[in_...  11.7 us
    ppermute x3, starting transfers between devices, per_device(): got = lax.ppermute(payload, 'leaf', routes[LEVELS - 1])  8.04 us
    ppermute x1, starting transfers between devices, per_device(): chip = sums + lax.ppermute(sums[0:1], 'leaf', routes[0])  6.95 us
    pallas_call x21, Pallas kernels, climb(): pl.pallas_call(functools.partial(climb_kernel, level), in_specs=[in_vmem]...  6.3 us
  transfers between devices with their start and end apart: 32, of which 25 were waited for; matrix products, arithmetic and copies ran while one was open for 0% of the time, Pallas kernels for 3%

profile of v1, /device:TPU:1, one launch (start us, length us, event | category | flops | bytes accessed | tf_op | source)
XLA Modules:
  0.0 170.2 jit_solution(16213158059808369510)
XLA Ops:
  2.5 3.4 %leaf_kernels.1._.kernel.rest_6_.rest_7_ = bf16[4,512,512]{2,1,0:T(8,128)(2,1)S(1)} custom-call(f32[28,2048]{1,0:T(8,128)S(1)} %copy-done.7, s32[1,2048]{1,0:T(1,128)S(1)} %copy-done.8), custom_call_target="tpu_custom_call" | custom-call | flops 1241513984 | bytes 4194304 | tf_op jit(solution)/shard_map/leaf_kernels/pallas_call | solution.py:137
  7.1 3.3 %collective-permute-start.1 = (bf16[256,256]{1,0:T(8,128)(2,1)S(1)}, bf16[256,256]{1,0:T(8,128)(2,1)S(1)}, u32[]{:S(2)}, u32[]{:S(2)}) collective-permute-start(bf16[256,256]{1,0:T(8,128)(2,1)S(1)} %get-tuple-element.80.step), channel_id=1, source_target_pairs={{0,1},{1,0},{2,3},{3,2},{4,5},{5,4},{6,7},{7,6},{8,9},{9,8},{10,11... | collective-permute-start | bytes 393224 | tf_op jit(solution)/shard_map/ppermute | solution.py:437
  20.4 4.4 %collective-permute-start.7 = (bf16[256,256]{1,0:T(8,128)(2,1)S(1)}, bf16[256,256]{1,0:T(8,128)(2,1)S(1)}, u32[]{:S(2)}, u32[]{:S(2)}) collective-permute-start(bf16[256,256]{1,0:T(8,128)(2,1)S(1)} %get-tuple-element.88.step), channel_id=1, source_target_pairs={{0,12},{1,13},{2,14},{3,15},{4,8},{5,9},{6,10},{7,11},{8,4},{9,5},... | collective-permute-start | bytes 393224 | tf_op jit(solution)/shard_map/ppermute | solution.py:437
  29.7 2.7 %collective-permute-done.6.got = bf16[272,128]{1,0:T(8,128)(2,1)S(1)} collective-permute-done((bf16[272,128]{1,0:T(8,128)(2,1)S(1)}, bf16[272,128]{1,0:T(8,128)(2,1)S(1)}, u32[]{:S(2)}, u32[]{:S(2)}) %collective-permute-start.6) | collective-permute-done | bytes 69664 | tf_op jit(solution)/shard_map/ppermute | solution.py:446
  36.5 2.6 %collective-permute-start.10 = (bf16[272,128]{1,0:T(8,128)(2,1)S(1)}, bf16[272,128]{1,0:T(8,128)(2,1)S(1)}, u32[]{:S(2)}, u32[]{:S(2)}) collective-permute-start(bf16[272,128]{1,0:T(8,128)(2,1)S(1)} %get-tuple-element.93.own), channel_id=1, source_target_pairs={{0,48},{1,49},{2,50},{3,51},{4,52},{5,53},{6,54},{7,55},{8,56},{9,... | collective-permute-start | bytes 208904 | tf_op jit(solution)/shard_map/ppermute | solution.py:446
  43.4 2.0 %collective-permute-done.12.got = bf16[272,128]{1,0:T(8,128)(2,1)S(1)} collective-permute-done((bf16[272,128]{1,0:T(8,128)(2,1)S(1)}, bf16[272,128]{1,0:T(8,128)(2,1)S(1)}, u32[]{:S(2)}, u32[]{:S(2)}) %collective-permute-start.12) | collective-permute-done | bytes 69664 | tf_op jit(solution)/shard_map/ppermute | solution.py:446
  45.7 2.6 %collective-permute-start.14 = (bf16[272,128]{1,0:T(8,128)(2,1)S(1)}, bf16[272,128]{1,0:T(8,128)(2,1)S(1)}, u32[]{:S(2)}, u32[]{:S(2)}) collective-permute-start(bf16[272,128]{1,0:T(8,128)(2,1)S(1)} %get-tuple-element.99.own), channel_id=1, source_target_pairs={{0,192},{1,193},{2,194},{3,195},{4,196},{5,197},{6,198},{7,199},{8... | collective-permute-start | bytes 208904 | tf_op jit(solution)/shard_map/ppermute | solution.py:450
  50.2 2.8 %turn.2 = (f32[2048,128]{1,0:T(8,128)S(1)}, f32[2048,128]{1,0:T(8,128)S(1)}, f32[2048,128]{1,0:T(8,128)S(1)}, f32[1024,128]{1,0:T(8,128)S(1)}, bf16[272,128]{1,0:T(8,128)(2,1)S(1)}, /*index=5*/f32[8,128]{1,0:T(8,128)S(1)}) custom-call(bf16[272,128]{1,0:T(8,128)(2,1)S(1)} %get-tuple-element.99.own, bf16[272,128]{1,0:T(8,128)(2,1)S(1)} %collective-permute-done.14.got, ...), custom_call_target="tpu_custom_call" | custom-call | tf_op jit(solution)/shard_map/turn/pallas_call | solution.py:86
  53.0 6.3 %collective-permute-start.15 = (bf16[272,128]{1,0:T(8,128)(2,1)S(1)}, bf16[272,128]{1,0:T(8,128)(2,1)S(1)}, u32[]{:S(2)}, u32[]{:S(2)}) collective-permute-start(bf16[272,128]{1,0:T(8,128)(2,1)S(1)} %get-tuple-element.104.own), channel_id=1, source_target_pairs={{0,1},{1,0},{2,3},{3,2},{4,5},{5,4},{6,7},{7,6},{8,9},{9,8},{10,11... | collective-permute-start | bytes 208904 | tf_op jit(solution)/shard_map/ppermute | solution.py:446
  62.4 2.3 %collective-permute-done.16.got = bf16[272,128]{1,0:T(8,128)(2,1)S(1)} collective-permute-done((bf16[272,128]{1,0:T(8,128)(2,1)S(1)}, bf16[272,128]{1,0:T(8,128)(2,1)S(1)}, u32[]{:S(2)}, u32[]{:S(2)}) %collective-permute-start.16) | collective-permute-done | bytes 69664 | tf_op jit(solution)/shard_map/ppermute | solution.py:446
  66.9 3.0 %collective-permute-done.17.got = bf16[272,128]{1,0:T(8,128)(2,1)S(1)} collective-permute-done((bf16[272,128]{1,0:T(8,128)(2,1)S(1)}, bf16[272,128]{1,0:T(8,128)(2,1)S(1)}, u32[]{:S(2)}, u32[]{:S(2)}) %collective-permute-start.17) | collective-permute-done | bytes 69664 | tf_op jit(solution)/shard_map/ppermute | solution.py:446
  70.2 2.5 %collective-permute-start.18 = (bf16[272,128]{1,0:T(8,128)(2,1)S(1)}, bf16[272,128]{1,0:T(8,128)(2,1)S(1)}, u32[]{:S(2)}, u32[]{:S(2)}) collective-permute-start(bf16[272,128]{1,0:T(8,128)(2,1)S(1)} %get-tuple-element.109.own), channel_id=1, source_target_pairs={{0,12},{1,13},{2,14},{3,15},{4,8},{5,9},{6,10},{7,11},{8,4},{9,5},... | collective-permute-start | bytes 208904 | tf_op jit(solution)/shard_map/ppermute | solution.py:446
  72.7 2.8 %collective-permute-done.18.got = bf16[272,128]{1,0:T(8,128)(2,1)S(1)} collective-permute-done((bf16[272,128]{1,0:T(8,128)(2,1)S(1)}, bf16[272,128]{1,0:T(8,128)(2,1)S(1)}, u32[]{:S(2)}, u32[]{:S(2)}) %collective-permute-start.18) | collective-permute-done | bytes 69664 | tf_op jit(solution)/shard_map/ppermute | solution.py:446
  75.9 3.1 %collective-permute-done.19.got = bf16[272,128]{1,0:T(8,128)(2,1)S(1)} collective-permute-done((bf16[272,128]{1,0:T(8,128)(2,1)S(1)}, bf16[272,128]{1,0:T(8,128)(2,1)S(1)}, u32[]{:S(2)}, u32[]{:S(2)}) %collective-permute-start.19) | collective-permute-done | bytes 69664 | tf_op jit(solution)/shard_map/ppermute | solution.py:446
  79.4 2.3 %collective-permute-start.20 = (bf16[272,128]{1,0:T(8,128)(2,1)S(1)}, bf16[272,128]{1,0:T(8,128)(2,1)S(1)}, u32[]{:S(2)}, u32[]{:S(2)}) collective-permute-start(bf16[272,128]{1,0:T(8,128)(2,1)S(1)} %get-tuple-element.113.own), channel_id=1, source_target_pairs={{0,48},{1,49},{2,50},{3,51},{4,52},{5,53},{6,54},{7,55},{8,56},{9,... | collective-permute-start | bytes 208904 | tf_op jit(solution)/shard_map/ppermute | solution.py:446
  81.7 2.2 %collective-permute-done.20.got = bf16[272,128]{1,0:T(8,128)(2,1)S(1)} collective-permute-done((bf16[272,128]{1,0:T(8,128)(2,1)S(1)}, bf16[272,128]{1,0:T(8,128)(2,1)S(1)}, u32[]{:S(2)}, u32[]{:S(2)}) %collective-permute-start.20) | collective-permute-done | bytes 69664 | tf_op jit(solution)/shard_map/ppermute | solution.py:446
  84.2 3.4 %collective-permute-done.21.got = bf16[272,128]{1,0:T(8,128)(2,1)S(1)} collective-permute-done((bf16[272,128]{1,0:T(8,128)(2,1)S(1)}, bf16[272,128]{1,0:T(8,128)(2,1)S(1)}, u32[]{:S(2)}, u32[]{:S(2)}) %collective-permute-start.21) | collective-permute-done | bytes 69664 | tf_op jit(solution)/shard_map/ppermute | solution.py:446
  88.0 2.8 %collective-permute-start.22 = (bf16[272,128]{1,0:T(8,128)(2,1)S(1)}, bf16[272,128]{1,0:T(8,128)(2,1)S(1)}, u32[]{:S(2)}, u32[]{:S(2)}) collective-permute-start(bf16[272,128]{1,0:T(8,128)(2,1)S(1)} %get-tuple-element.117.own), channel_id=1, source_target_pairs={{0,192},{1,193},{2,194},{3,195},{4,196},{5,197},{6,198},{7,199},{8... | collective-permute-start | bytes 208904 | tf_op jit(solution)/shard_map/ppermute | solution.py:450
  92.7 2.8 %turn.3 = (f32[2048,128]{1,0:T(8,128)S(1)}, f32[2048,128]{1,0:T(8,128)S(1)}, f32[2048,128]{1,0:T(8,128)S(1)}, f32[2048,128]{1,0:T(8,128)S(1)}, f32[1024,128]{1,0...) custom-call(bf16[272,128]{1,0:T(8,128)(2,1)S(1)} %get-tuple-element.117.own, ...), custom_call_target="tpu_custom_call" | custom-call | tf_op jit(solution)/shard_map/turn/pallas_call | solution.py:86
  95.5 7.0 %collective-permute-start.23 = (bf16[272,128]{1,0:T(8,128)(2,1)S(1)}, bf16[272,128]{1,0:T(8,128)(2,1)S(1)}, u32[]{:S(2)}, u32[]{:S(2)}) collective-permute-start(bf16[272,128]{1,0:T(8,128)(2,1)S(1)} %get-tuple-element.124.own), channel_id=1, source_target_pairs={{0,1},{1,0},{2,3},{3,2},{4,5},{5,4},{6,7},{7,6},{8,9},{9,8},{10,11... | collective-permute-start | bytes 208904 | tf_op jit(solution)/shard_map/ppermute | solution.py:446
  105.7 2.3 %collective-permute-done.24.got = bf16[272,128]{1,0:T(8,128)(2,1)S(1)} collective-permute-done((bf16[272,128]{1,0:T(8,128)(2,1)S(1)}, bf16[272,128]{1,0:T(8,128)(2,1)S(1)}, u32[]{:S(2)}, u32[]{:S(2)}) %collective-permute-start.24) | collective-permute-done | bytes 69664 | tf_op jit(solution)/shard_map/ppermute | solution.py:446
  110.0 3.1 %collective-permute-done.25.got = bf16[272,128]{1,0:T(8,128)(2,1)S(1)} collective-permute-done((bf16[272,128]{1,0:T(8,128)(2,1)S(1)}, bf16[272,128]{1,0:T(8,128)(2,1)S(1)}, u32[]{:S(2)}, u32[]{:S(2)}) %collective-permute-start.25) | collective-permute-done | bytes 69664 | tf_op jit(solution)/shard_map/ppermute | solution.py:446
  113.4 2.4 %collective-permute-start.26 = (bf16[272,128]{1,0:T(8,128)(2,1)S(1)}, bf16[272,128]{1,0:T(8,128)(2,1)S(1)}, u32[]{:S(2)}, u32[]{:S(2)}) collective-permute-start(bf16[272,128]{1,0:T(8,128)(2,1)S(1)} %get-tuple-element.129.own), channel_id=1, source_target_pairs={{0,12},{1,13},{2,14},{3,15},{4,8},{5,9},{6,10},{7,11},{8,4},{9,5},... | collective-permute-start | bytes 208904 | tf_op jit(solution)/shard_map/ppermute | solution.py:446
  115.8 3.0 %collective-permute-done.26.got = bf16[272,128]{1,0:T(8,128)(2,1)S(1)} collective-permute-done((bf16[272,128]{1,0:T(8,128)(2,1)S(1)}, bf16[272,128]{1,0:T(8,128)(2,1)S(1)}, u32[]{:S(2)}, u32[]{:S(2)}) %collective-permute-start.26) | collective-permute-done | bytes 69664 | tf_op jit(solution)/shard_map/ppermute | solution.py:446
  119.2 3.1 %collective-permute-done.27.got = bf16[272,128]{1,0:T(8,128)(2,1)S(1)} collective-permute-done((bf16[272,128]{1,0:T(8,128)(2,1)S(1)}, bf16[272,128]{1,0:T(8,128)(2,1)S(1)}, u32[]{:S(2)}, u32[]{:S(2)}) %collective-permute-start.27) | collective-permute-done | bytes 69664 | tf_op jit(solution)/shard_map/ppermute | solution.py:446
  122.6 2.4 %collective-permute-start.28 = (bf16[272,128]{1,0:T(8,128)(2,1)S(1)}, bf16[272,128]{1,0:T(8,128)(2,1)S(1)}, u32[]{:S(2)}, u32[]{:S(2)}) collective-permute-start(bf16[272,128]{1,0:T(8,128)(2,1)S(1)} %get-tuple-element.133.own), channel_id=1, source_target_pairs={{0,48},{1,49},{2,50},{3,51},{4,52},{5,53},{6,54},{7,55},{8,56},{9,... | collective-permute-start | bytes 208904 | tf_op jit(solution)/shard_map/ppermute | solution.py:446
  125.0 2.1 %collective-permute-done.28.got = bf16[272,128]{1,0:T(8,128)(2,1)S(1)} collective-permute-done((bf16[272,128]{1,0:T(8,128)(2,1)S(1)}, bf16[272,128]{1,0:T(8,128)(2,1)S(1)}, u32[]{:S(2)}, u32[]{:S(2)}) %collective-permute-start.28) | collective-permute-done | bytes 69664 | tf_op jit(solution)/shard_map/ppermute | solution.py:446
  127.5 3.4 %collective-permute-done.29.got = bf16[272,128]{1,0:T(8,128)(2,1)S(1)} collective-permute-done((bf16[272,128]{1,0:T(8,128)(2,1)S(1)}, bf16[272,128]{1,0:T(8,128)(2,1)S(1)}, u32[]{:S(2)}, u32[]{:S(2)}) %collective-permute-start.29) | collective-permute-done | bytes 69664 | tf_op jit(solution)/shard_map/ppermute | solution.py:446
  131.2 2.6 %collective-permute-start.30 = (bf16[272,128]{1,0:T(8,128)(2,1)S(1)}, bf16[272,128]{1,0:T(8,128)(2,1)S(1)}, u32[]{:S(2)}, u32[]{:S(2)}) collective-permute-start(bf16[272,128]{1,0:T(8,128)(2,1)S(1)} %get-tuple-element.137.own), channel_id=1, source_target_pairs={{0,192},{1,193},{2,194},{3,195},{4,196},{5,197},{6,198},{7,199},{8... | collective-permute-start | bytes 208904 | tf_op jit(solution)/shard_map/ppermute | solution.py:450
  135.7 2.3 %end.1 = (f32[2048,128]{1,0:T(8,128)}, f32[2048,128]{1,0:T(8,128)S(1)}, f32[2048,128]{1,0:T(8,128)S(1)}, f32[2048,128]{1,0:T(8,128)}, f32[8,128]{1,0:T(8,128)S(1)}, /*index=5*/f32[128,128]{1,0:T(8,128)S(1)}) custom-call(bf16[272,128]{1,0:T(8,128)(2,1)S(1)} %get-tuple-element.137.own, bf16[272,128]{1,0:T(8,128)(2,1)S(1)} %collective-permute-done.30.got, ...), custom_call_target="tpu_custom_call" | custom-call | tf_op jit(solution)/shard_map/end/pallas_call | solution.py:86
  138.0 6.9 %collective-permute-start.31 = (f32[1,128]{1,0:T(1,128)S(1)}, f32[1,128]{1,0:T(1,128)S(1)}, u32[]{:S(2)}, u32[]{:S(2)}) collective-permute-start(f32[1,128]{1,0:T(1,128)S(1)} %slice.11), channel_id=1, source_target_pairs={{0,1},{1,0},{2,3},{3,2},{4,5},{5,4},{6,7},{7,6},{8,9},{9,8},{10,11... | collective-permute-start | bytes 1544 | tf_op jit(solution)/shard_map/ppermute | solution.py:462
  145.8 23.3 %all_to_all.11 = f32[128,1,128]{2,1,0:T(1,128)S(1)} all-to-all(f32[128,1,128]{2,1,0:T(1,128)S(1)} %bitcast.10), channel_id=1, replica_groups={{0,2,4,6,8,10,12,14,16,18,20,22,24,26,28,30,32,34,36,38,40,42,44,46,48,..., dimensions={0} | all-to-all | bytes 131072 | tf_op jit(solution)/shard_map/all_to_all | solution.py:464
  (88 shorter events, 47.9 us)
Async XLA Ops:
  7.1 6.5 %collective-permute-start.1 = (bf16[256,256]{1,0:T(8,128)(2,1)S(1)}, bf16[256,256]{1,0:T(8,128)(2,1)S(1)}, u32[]{:S(2)}, u32[]{:S(2)}) collective-permute-start(bf16[256,256]{1,0:T(8,128)(2,1)S(1)} %get-tuple-element.80.step), channel_id=1, source_target_pairs={{0,1},{1,0},{2,3},{3,2},{4,5},{5,4},{6,7},{7,6},{8,9},{9,8},{10,11... | collective-permute-start | bytes 393224 | tf_op jit(solution)/shard_map/ppermute | solution.py:437
  12.2 1.4 collective-permute-start
  12.6 4.9 %collective-permute-start.3 = (bf16[256,256]{1,0:T(8,128)(2,1)S(1)}, bf16[256,256]{1,0:T(8,128)(2,1)S(1)}, u32[]{:S(2)}, u32[]{:S(2)}) collective-permute-start(bf16[256,256]{1,0:T(8,128)(2,1)S(1)} %get-tuple-element.82.step), channel_id=1, source_target_pairs={{0,2},{1,3},{2,0},{3,1},{4,6},{5,7},{6,4},{7,5},{8,10},{9,11},{10,... | collective-permute-start | bytes 393224 | tf_op jit(solution)/shard_map/ppermute | solution.py:437
  13.9 5.1 %collective-permute-start.2 = (bf16[272,128]{1,0:T(8,128)(2,1)S(1)}, bf16[272,128]{1,0:T(8,128)(2,1)S(1)}, u32[]{:S(2)}, u32[]{:S(2)}) collective-permute-start(bf16[272,128]{1,0:T(8,128)(2,1)S(1)} %get-tuple-element.81.own), channel_id=1, source_target_pairs={{0,2},{1,3},{2,0},{3,1},{4,6},{5,7},{6,4},{7,5},{8,10},{9,11},{10,... | collective-permute-start | bytes 208904 | tf_op jit(solution)/shard_map/ppermute | solution.py:446
  15.4 9.4 %collective-permute-start.5 = (bf16[256,256]{1,0:T(8,128)(2,1)S(1)}, bf16[256,256]{1,0:T(8,128)(2,1)S(1)}, u32[]{:S(2)}, u32[]{:S(2)}) collective-permute-start(bf16[256,256]{1,0:T(8,128)(2,1)S(1)} %get-tuple-element.85.step), channel_id=1, source_target_pairs={{0,4},{1,5},{2,6},{3,7},{4,0},{5,1},{6,2},{7,3},{8,12},{9,13},{10,... | collective-permute-start | bytes 393224 | tf_op jit(solution)/shard_map/ppermute | solution.py:437
  19.2 7.3 %collective-permute-start.4 = (bf16[272,128]{1,0:T(8,128)(2,1)S(1)}, bf16[272,128]{1,0:T(8,128)(2,1)S(1)}, u32[]{:S(2)}, u32[]{:S(2)}) collective-permute-start(bf16[272,128]{1,0:T(8,128)(2,1)S(1)} %get-tuple-element.84.own), channel_id=1, source_target_pairs={{0,4},{1,5},{2,6},{3,7},{4,0},{5,1},{6,2},{7,3},{8,12},{9,13},{10,... | collective-permute-start | bytes 208904 | tf_op jit(solution)/shard_map/ppermute | solution.py:446
  20.4 9.3 %collective-permute-start.7 = (bf16[256,256]{1,0:T(8,128)(2,1)S(1)}, bf16[256,256]{1,0:T(8,128)(2,1)S(1)}, u32[]{:S(2)}, u32[]{:S(2)}) collective-permute-start(bf16[256,256]{1,0:T(8,128)(2,1)S(1)} %get-tuple-element.88.step), channel_id=1, source_target_pairs={{0,12},{1,13},{2,14},{3,15},{4,8},{5,9},{6,10},{7,11},{8,4},{9,5},... | collective-permute-start | bytes 393224 | tf_op jit(solution)/shard_map/ppermute | solution.py:437
  26.9 5.5 %collective-permute-start.6 = (bf16[272,128]{1,0:T(8,128)(2,1)S(1)}, bf16[272,128]{1,0:T(8,128)(2,1)S(1)}, u32[]{:S(2)}, u32[]{:S(2)}) collective-permute-start(bf16[272,128]{1,0:T(8,128)(2,1)S(1)} %get-tuple-element.87.own), channel_id=1, source_target_pairs={{0,12},{1,13},{2,14},{3,15},{4,8},{5,9},{6,10},{7,11},{8,4},{9,5},... | collective-permute-start | bytes 208904 | tf_op jit(solution)/shard_map/ppermute | solution.py:446
  28.4 7.5 %collective-permute-start.9 = (bf16[256,256]{1,0:T(8,128)(2,1)S(1)}, bf16[256,256]{1,0:T(8,128)(2,1)S(1)}, u32[]{:S(2)}, u32[]{:S(2)}) collective-permute-start(bf16[256,256]{1,0:T(8,128)(2,1)S(1)} %get-tuple-element.91.step), channel_id=1, source_target_pairs={{0,16},{1,17},{2,18},{3,19},{4,20},{5,21},{6,22},{7,23},{8,24},{9,... | collective-permute-start | bytes 393224 | tf_op jit(solution)/shard_map/ppermute | solution.py:437
  32.6 3.6 %collective-permute-start.8 = (bf16[272,128]{1,0:T(8,128)(2,1)S(1)}, bf16[272,128]{1,0:T(8,128)(2,1)S(1)}, u32[]{:S(2)}, u32[]{:S(2)}) collective-permute-start(bf16[272,128]{1,0:T(8,128)(2,1)S(1)} %get-tuple-element.90.own), channel_id=1, source_target_pairs={{0,16},{1,17},{2,18},{3,19},{4,20},{5,21},{6,22},{7,23},{8,24},{9,... | collective-permute-start | bytes 208904 | tf_op jit(solution)/shard_map/ppermute | solution.py:446
  34.1 6.3 %collective-permute-start.11 = (bf16[256,256]{1,0:T(8,128)(2,1)S(1)}, bf16[256,256]{1,0:T(8,128)(2,1)S(1)}, u32[]{:S(2)}, u32[]{:S(2)}) collective-permute-start(bf16[256,256]{1,0:T(8,128)(2,1)S(1)} %get-tuple-element.94.step), channel_id=1, source_target_pairs={{0,48},{1,49},{2,50},{3,51},{4,52},{5,53},{6,54},{7,55},{8,56},{9,... | collective-permute-start | bytes 393224 | tf_op jit(solution)/shard_map/ppermute | solution.py:437
  36.5 5.2 %collective-permute-start.10 = (bf16[272,128]{1,0:T(8,128)(2,1)S(1)}, bf16[272,128]{1,0:T(8,128)(2,1)S(1)}, u32[]{:S(2)}, u32[]{:S(2)}) collective-permute-start(bf16[272,128]{1,0:T(8,128)(2,1)S(1)} %get-tuple-element.93.own), channel_id=1, source_target_pairs={{0,48},{1,49},{2,50},{3,51},{4,52},{5,53},{6,54},{7,55},{8,56},{9,... | collective-permute-start | bytes 208904 | tf_op jit(solution)/shard_map/ppermute | solution.py:446
  39.1 4.3 %collective-permute-start.13 = (bf16[256,256]{1,0:T(8,128)(2,1)S(1)}, bf16[256,256]{1,0:T(8,128)(2,1)S(1)}, u32[]{:S(2)}, u32[]{:S(2)}) collective-permute-start(bf16[256,256]{1,0:T(8,128)(2,1)S(1)} %get-tuple-element.97.step), channel_id=1, source_target_pairs={{0,64},{1,65},{2,66},{3,67},{4,68},{5,69},{6,70},{7,71},{8,72},{9,... | collective-permute-start | bytes 393224 | tf_op jit(solution)/shard_map/ppermute | solution.py:437
  42.0 3.4 %collective-permute-start.12 = (bf16[272,128]{1,0:T(8,128)(2,1)S(1)}, bf16[272,128]{1,0:T(8,128)(2,1)S(1)}, u32[]{:S(2)}, u32[]{:S(2)}) collective-permute-start(bf16[272,128]{1,0:T(8,128)(2,1)S(1)} %get-tuple-element.96.own), channel_id=1, source_target_pairs={{0,64},{1,65},{2,66},{3,67},{4,68},{5,69},{6,70},{7,71},{8,72},{9,... | collective-permute-start | bytes 208904 | tf_op jit(solution)/shard_map/ppermute | solution.py:446
  45.7 4.5 %collective-permute-start.14 = (bf16[272,128]{1,0:T(8,128)(2,1)S(1)}, bf16[272,128]{1,0:T(8,128)(2,1)S(1)}, u32[]{:S(2)}, u32[]{:S(2)}) collective-permute-start(bf16[272,128]{1,0:T(8,128)(2,1)S(1)} %get-tuple-element.99.own), channel_id=1, source_target_pairs={{0,192},{1,193},{2,194},{3,195},{4,196},{5,197},{6,198},{7,199},{8... | collective-permute-start | bytes 208904 | tf_op jit(solution)/shard_map/ppermute | solution.py:450
  53.0 7.2 %collective-permute-start.15 = (bf16[272,128]{1,0:T(8,128)(2,1)S(1)}, bf16[272,128]{1,0:T(8,128)(2,1)S(1)}, u32[]{:S(2)}, u32[]{:S(2)}) collective-permute-start(bf16[272,128]{1,0:T(8,128)(2,1)S(1)} %get-tuple-element.104.own), channel_id=1, source_target_pairs={{0,1},{1,0},{2,3},{3,2},{4,5},{5,4},{6,7},{7,6},{8,9},{9,8},{10,11... | collective-permute-start | bytes 208904 | tf_op jit(solution)/shard_map/ppermute | solution.py:446
  60.5 4.2 %collective-permute-start.16 = (bf16[272,128]{1,0:T(8,128)(2,1)S(1)}, bf16[272,128]{1,0:T(8,128)(2,1)S(1)}, u32[]{:S(2)}, u32[]{:S(2)}) collective-permute-start(bf16[272,128]{1,0:T(8,128)(2,1)S(1)} %get-tuple-element.105.own), channel_id=1, source_target_pairs={{0,2},{1,3},{2,0},{3,1},{4,6},{5,7},{6,4},{7,5},{8,10},{9,11},{10,... | collective-permute-start | bytes 208904 | tf_op jit(solution)/shard_map/ppermute | solution.py:446
  65.0 4.9 %collective-permute-start.17 = (bf16[272,128]{1,0:T(8,128)(2,1)S(1)}, bf16[272,128]{1,0:T(8,128)(2,1)S(1)}, u32[]{:S(2)}, u32[]{:S(2)}) collective-permute-start(bf16[272,128]{1,0:T(8,128)(2,1)S(1)} %get-tuple-element.107.own), channel_id=1, source_target_pairs={{0,4},{1,5},{2,6},{3,7},{4,0},{5,1},{6,2},{7,3},{8,12},{9,13},{10,... | collective-permute-start | bytes 208904 | tf_op jit(solution)/shard_map/ppermute | solution.py:446
  70.2 5.4 %collective-permute-start.18 = (bf16[272,128]{1,0:T(8,128)(2,1)S(1)}, bf16[272,128]{1,0:T(8,128)(2,1)S(1)}, u32[]{:S(2)}, u32[]{:S(2)}) collective-permute-start(bf16[272,128]{1,0:T(8,128)(2,1)S(1)} %get-tuple-element.109.own), channel_id=1, source_target_pairs={{0,12},{1,13},{2,14},{3,15},{4,8},{5,9},{6,10},{7,11},{8,4},{9,5},... | collective-permute-start | bytes 208904 | tf_op jit(solution)/shard_map/ppermute | solution.py:446
  75.8 3.2 %collective-permute-start.19 = (bf16[272,128]{1,0:T(8,128)(2,1)S(1)}, bf16[272,128]{1,0:T(8,128)(2,1)S(1)}, u32[]{:S(2)}, u32[]{:S(2)}) collective-permute-start(bf16[272,128]{1,0:T(8,128)(2,1)S(1)} %get-tuple-element.111.own), channel_id=1, source_target_pairs={{0,16},{1,17},{2,18},{3,19},{4,20},{5,21},{6,22},{7,23},{8,24},{9,... | collective-permute-start | bytes 208904 | tf_op jit(solution)/shard_map/ppermute | solution.py:446
  79.4 4.5 %collective-permute-start.20 = (bf16[272,128]{1,0:T(8,128)(2,1)S(1)}, bf16[272,128]{1,0:T(8,128)(2,1)S(1)}, u32[]{:S(2)}, u32[]{:S(2)}) collective-permute-start(bf16[272,128]{1,0:T(8,128)(2,1)S(1)} %get-tuple-element.113.own), channel_id=1, source_target_pairs={{0,48},{1,49},{2,50},{3,51},{4,52},{5,53},{6,54},{7,55},{8,56},{9,... | collective-permute-start | bytes 208904 | tf_op jit(solution)/shard_map/ppermute | solution.py:446
  84.1 3.5 %collective-permute-start.21 = (bf16[272,128]{1,0:T(8,128)(2,1)S(1)}, bf16[272,128]{1,0:T(8,128)(2,1)S(1)}, u32[]{:S(2)}, u32[]{:S(2)}) collective-permute-start(bf16[272,128]{1,0:T(8,128)(2,1)S(1)} %get-tuple-element.115.own), channel_id=1, source_target_pairs={{0,64},{1,65},{2,66},{3,67},{4,68},{5,69},{6,70},{7,71},{8,72},{9,... | collective-permute-start | bytes 208904 | tf_op jit(solution)/shard_map/ppermute | solution.py:446
  88.0 4.7 %collective-permute-start.22 = (bf16[272,128]{1,0:T(8,128)(2,1)S(1)}, bf16[272,128]{1,0:T(8,128)(2,1)S(1)}, u32[]{:S(2)}, u32[]{:S(2)}) collective-permute-start(bf16[272,128]{1,0:T(8,128)(2,1)S(1)} %get-tuple-element.117.own), channel_id=1, source_target_pairs={{0,192},{1,193},{2,194},{3,195},{4,196},{5,197},{6,198},{7,199},{8... | collective-permute-start | bytes 208904 | tf_op jit(solution)/shard_map/ppermute | solution.py:450
  95.5 8.0 %collective-permute-start.23 = (bf16[272,128]{1,0:T(8,128)(2,1)S(1)}, bf16[272,128]{1,0:T(8,128)(2,1)S(1)}, u32[]{:S(2)}, u32[]{:S(2)}) collective-permute-start(bf16[272,128]{1,0:T(8,128)(2,1)S(1)} %get-tuple-element.124.own), channel_id=1, source_target_pairs={{0,1},{1,0},{2,3},{3,2},{4,5},{5,4},{6,7},{7,6},{8,9},{9,8},{10,11... | collective-permute-start | bytes 208904 | tf_op jit(solution)/shard_map/ppermute | solution.py:446
  103.7 4.2 %collective-permute-start.24 = (bf16[272,128]{1,0:T(8,128)(2,1)S(1)}, bf16[272,128]{1,0:T(8,128)(2,1)S(1)}, u32[]{:S(2)}, u32[]{:S(2)}) collective-permute-start(bf16[272,128]{1,0:T(8,128)(2,1)S(1)} %get-tuple-element.125.own), channel_id=1, source_target_pairs={{0,2},{1,3},{2,0},{3,1},{4,6},{5,7},{6,4},{7,5},{8,10},{9,11},{10,... | collective-permute-start | bytes 208904 | tf_op jit(solution)/shard_map/ppermute | solution.py:446
  108.2 4.9 %collective-permute-start.25 = (bf16[272,128]{1,0:T(8,128)(2,1)S(1)}, bf16[272,128]{1,0:T(8,128)(2,1)S(1)}, u32[]{:S(2)}, u32[]{:S(2)}) collective-permute-start(bf16[272,128]{1,0:T(8,128)(2,1)S(1)} %get-tuple-element.127.own), channel_id=1, source_target_pairs={{0,4},{1,5},{2,6},{3,7},{4,0},{5,1},{6,2},{7,3},{8,12},{9,13},{10,... | collective-permute-start | bytes 208904 | tf_op jit(solution)/shard_map/ppermute | solution.py:446
  113.4 5.4 %collective-permute-start.26 = (bf16[272,128]{1,0:T(8,128)(2,1)S(1)}, bf16[272,128]{1,0:T(8,128)(2,1)S(1)}, u32[]{:S(2)}, u32[]{:S(2)}) collective-permute-start(bf16[272,128]{1,0:T(8,128)(2,1)S(1)} %get-tuple-element.129.own), channel_id=1, source_target_pairs={{0,12},{1,13},{2,14},{3,15},{4,8},{5,9},{6,10},{7,11},{8,4},{9,5},... | collective-permute-start | bytes 208904 | tf_op jit(solution)/shard_map/ppermute | solution.py:446
  119.1 3.2 %collective-permute-start.27 = (bf16[272,128]{1,0:T(8,128)(2,1)S(1)}, bf16[272,128]{1,0:T(8,128)(2,1)S(1)}, u32[]{:S(2)}, u32[]{:S(2)}) collective-permute-start(bf16[272,128]{1,0:T(8,128)(2,1)S(1)} %get-tuple-element.131.own), channel_id=1, source_target_pairs={{0,16},{1,17},{2,18},{3,19},{4,20},{5,21},{6,22},{7,23},{8,24},{9,... | collective-permute-start | bytes 208904 | tf_op jit(solution)/shard_map/ppermute | solution.py:446
  122.6 4.5 %collective-permute-start.28 = (bf16[272,128]{1,0:T(8,128)(2,1)S(1)}, bf16[272,128]{1,0:T(8,128)(2,1)S(1)}, u32[]{:S(2)}, u32[]{:S(2)}) collective-permute-start(bf16[272,128]{1,0:T(8,128)(2,1)S(1)} %get-tuple-element.133.own), channel_id=1, source_target_pairs={{0,48},{1,49},{2,50},{3,51},{4,52},{5,53},{6,54},{7,55},{8,56},{9,... | collective-permute-start | bytes 208904 | tf_op jit(solution)/shard_map/ppermute | solution.py:446
  127.4 3.5 %collective-permute-start.29 = (bf16[272,128]{1,0:T(8,128)(2,1)S(1)}, bf16[272,128]{1,0:T(8,128)(2,1)S(1)}, u32[]{:S(2)}, u32[]{:S(2)}) collective-permute-start(bf16[272,128]{1,0:T(8,128)(2,1)S(1)} %get-tuple-element.135.own), channel_id=1, source_target_pairs={{0,64},{1,65},{2,66},{3,67},{4,68},{5,69},{6,70},{7,71},{8,72},{9,... | collective-permute-start | bytes 208904 | tf_op jit(solution)/shard_map/ppermute | solution.py:446
  131.2 4.5 %collective-permute-start.30 = (bf16[272,128]{1,0:T(8,128)(2,1)S(1)}, bf16[272,128]{1,0:T(8,128)(2,1)S(1)}, u32[]{:S(2)}, u32[]{:S(2)}) collective-permute-start(bf16[272,128]{1,0:T(8,128)(2,1)S(1)} %get-tuple-element.137.own), channel_id=1, source_target_pairs={{0,192},{1,193},{2,194},{3,195},{4,196},{5,197},{6,198},{7,199},{8... | collective-permute-start | bytes 208904 | tf_op jit(solution)/shard_map/ppermute | solution.py:450
  138.0 7.8 %collective-permute-start.31 = (f32[1,128]{1,0:T(1,128)S(1)}, f32[1,128]{1,0:T(1,128)S(1)}, u32[]{:S(2)}, u32[]{:S(2)}) collective-permute-start(f32[1,128]{1,0:T(1,128)S(1)} %slice.11), channel_id=1, source_target_pairs={{0,1},{1,0},{2,3},{3,2},{4,5},{5,4},{6,7},{7,6},{8,9},{9,8},{10,11... | collective-permute-start | bytes 1544 | tf_op jit(solution)/shard_map/ppermute | solution.py:462
  (10 other events, 40.8 us)

commit v2 on v1

--- a/solution.py
+++ b/solution.py
@@ -222,7 +222,10 @@
     mine = own[:RANK]
     theirs = got[:RANK]
     out[:RANK] = (dot(step[...], mine) + dot(other[...], theirs)).astype(BF)
-    felt = dot(down[level], theirs)
+    if level:
+        felt = dot(down[level], theirs)
+    else:
+        felt = dot(down[0, 0], theirs)
     energy = jnp.sum(mine.astype(F32) * felt[:RANK], axis=0, keepdims=True)
     zero = jnp.zeros_like(energy)
     sums = unpack_sums(own[RANK:]) + unpack_sums(got[RANK:])
@@ -230,7 +233,7 @@
     if level:
         field_out[...] = field_in[...] + felt[RANK:]
     else:
-        field_out[...] = felt[RANK:]
+        field_out[...] = felt
 
 
 def climb(level, own, got, step, other, down, field):
@@ -444,8 +447,9 @@
         field = None
         for level in range(LEVELS - 1):
             got = lax.ppermute(payload, "leaf", routes[level])
+            across = down if level else device_coupling
             payload, field = climb(
-                level, payload, got, steps[level], others[level], down, field
+                level, payload, got, steps[level], others[level], across, field
             )
         got = lax.ppermute(payload, "leaf", routes[LEVELS - 1])
         sweep = (payload, got, down, field)

time: 170 us -> 171 us (level)
  starting transfers between devices: 69.5 us -> 73.8 us
  waiting for transfers between devices: 51.9 us -> 48.7 us
    ppermute x21, waiting for transfers between devices: 45.2 us -> 40.9 us  [per_device(): got = lax.ppermute(payload, 'leaf', routes[level])]
  transfers between devices with their start and end apart: 32 -> 32, of which waited for: 25 -> 26; matrix products, arithmetic and copies ran while one was open for 0% -> 0% of each run, Pallas kernels for 3% -> 3%
where the time goes in v2:
time: 171 us
  starting transfers between devices  73.8 us (43%)
  waiting for transfers between devices  48.7 us (28%)
  blocking collectives  23.2 us (14%)
  Pallas kernels  22.5 us (13%)
  local copies, waits for them, and re-layouts  1.84 us (1%)
    ppermute x21, starting transfers between devices, per_device(): got = lax.ppermute(payload, 'leaf', routes[level])  42 us
    ppermute x21, waiting for transfers between devices, per_device(): got = lax.ppermute(payload, 'leaf', routes[level])  40.9 us
    all_to_all x1, blocking collectives, per_device(): lax.all_to_all(chip, 'leaf', 0, 0, axis_index_groups=same_core, tiled=True)  23.2 us
    ppermute x7, starting transfers between devices, per_device(): lax.ppermute(block, 'leaf', route)  15.1 us
    pallas_call x6, Pallas kernels, call(): pl.pallas_call(kernel, in_specs=[in_vmem] * len(operands), out_specs=[in_...  11.8 us
    ppermute x3, starting transfers between devices, per_device(): got = lax.ppermute(payload, 'leaf', routes[LEVELS - 1])  8.71 us
    ppermute x1, starting transfers between devices, per_device(): chip = sums + lax.ppermute(sums[0:1], 'leaf', routes[0])  8.01 us
    pallas_call x21, Pallas kernels, climb(): pl.pallas_call(functools.partial(climb_kernel, level), in_specs=[in_vmem]...  6.17 us
  transfers between devices with their start and end apart: 32, of which 26 were waited for; matrix products, arithmetic and copies ran while one was open for 0% of the time, Pallas kernels for 3%

profile of v2, /device:TPU:1, one launch (start us, length us, event | category | flops | bytes accessed | tf_op | source)
XLA Modules:
  0.0 171.1 jit_solution(6822604604243870267)
XLA Ops:
  2.5 3.4 %leaf_kernels.1._.kernel.rest_6_.rest_7_ = bf16[4,512,512]{2,1,0:T(8,128)(2,1)S(1)} custom-call(f32[28,2048]{1,0:T(8,128)S(1)} %copy-done.7, s32[1,2048]{1,0:T(1,128)S(1)} %copy-done.8), custom_call_target="tpu_custom_call" | custom-call | flops 1241513984 | bytes 4194304 | tf_op jit(solution)/shard_map/leaf_kernels/pallas_call | solution.py:137
  7.1 3.3 %collective-permute-start.1 = (bf16[256,256]{1,0:T(8,128)(2,1)S(1)}, bf16[256,256]{1,0:T(8,128)(2,1)S(1)}, u32[]{:S(2)}, u32[]{:S(2)}) collective-permute-start(bf16[256,256]{1,0:T(8,128)(2,1)S(1)} %get-tuple-element.80.step), channel_id=1, source_target_pairs={{0,1},{1,0},{2,3},{3,2},{4,5},{5,4},{6,7},{7,6},{8,9},{9,8},{10,11... | collective-permute-start | bytes 393224 | tf_op jit(solution)/shard_map/ppermute | solution.py:440
  14.4 2.4 %collective-permute-start.5 = (bf16[256,256]{1,0:T(8,128)(2,1)S(1)}, bf16[256,256]{1,0:T(8,128)(2,1)S(1)}, u32[]{:S(2)}, u32[]{:S(2)}) collective-permute-start(bf16[256,256]{1,0:T(8,128)(2,1)S(1)} %get-tuple-element.85.step), channel_id=1, source_target_pairs={{0,4},{1,5},{2,6},{3,7},{4,0},{5,1},{6,2},{7,3},{8,12},{9,13},{10,... | collective-permute-start | bytes 393224 | tf_op jit(solution)/shard_map/ppermute | solution.py:440
  17.8 3.9 %collective-permute-done.2.got = bf16[272,128]{1,0:T(8,128)(2,1)S(1)} collective-permute-done((bf16[272,128]{1,0:T(8,128)(2,1)S(1)}, bf16[272,128]{1,0:T(8,128)(2,1)S(1)}, u32[]{:S(2)}, u32[]{:S(2)}) %collective-permute-start.2) | collective-permute-done | bytes 69664 | tf_op jit(solution)/shard_map/ppermute | solution.py:449
  22.1 5.0 %collective-permute-start.7 = (bf16[256,256]{1,0:T(8,128)(2,1)S(1)}, bf16[256,256]{1,0:T(8,128)(2,1)S(1)}, u32[]{:S(2)}, u32[]{:S(2)}) collective-permute-start(bf16[256,256]{1,0:T(8,128)(2,1)S(1)} %get-tuple-element.88.step), channel_id=1, source_target_pairs={{0,12},{1,13},{2,14},{3,15},{4,8},{5,9},{6,10},{7,11},{8,4},{9,5},... | collective-permute-start | bytes 393224 | tf_op jit(solution)/shard_map/ppermute | solution.py:440
  30.4 2.0 %collective-permute-done.7.other = bf16[256,256]{1,0:T(8,128)(2,1)S(1)} collective-permute-done((bf16[256,256]{1,0:T(8,128)(2,1)S(1)}, bf16[256,256]{1,0:T(8,128)(2,1)S(1)}, u32[]{:S(2)}, u32[]{:S(2)}) %collective-permute-start.7) | collective-permute-done | bytes 131104 | tf_op jit(solution)/shard_map/ppermute | solution.py:440
  32.4 3.0 %collective-permute-done.6.got = bf16[272,128]{1,0:T(8,128)(2,1)S(1)} collective-permute-done((bf16[272,128]{1,0:T(8,128)(2,1)S(1)}, bf16[272,128]{1,0:T(8,128)(2,1)S(1)}, u32[]{:S(2)}, u32[]{:S(2)}) %collective-permute-start.6) | collective-permute-done | bytes 69664 | tf_op jit(solution)/shard_map/ppermute | solution.py:449
  39.4 2.6 %collective-permute-start.10 = (bf16[272,128]{1,0:T(8,128)(2,1)S(1)}, bf16[272,128]{1,0:T(8,128)(2,1)S(1)}, u32[]{:S(2)}, u32[]{:S(2)}) collective-permute-start(bf16[272,128]{1,0:T(8,128)(2,1)S(1)} %get-tuple-element.93.own), channel_id=1, source_target_pairs={{0,48},{1,49},{2,50},{3,51},{4,52},{5,53},{6,54},{7,55},{8,56},{9,... | collective-permute-start | bytes 208904 | tf_op jit(solution)/shard_map/ppermute | solution.py:449
  46.1 2.8 %collective-permute-done.12.got = bf16[272,128]{1,0:T(8,128)(2,1)S(1)} collective-permute-done((bf16[272,128]{1,0:T(8,128)(2,1)S(1)}, bf16[272,128]{1,0:T(8,128)(2,1)S(1)}, u32[]{:S(2)}, u32[]{:S(2)}) %collective-permute-start.12) | collective-permute-done | bytes 69664 | tf_op jit(solution)/shard_map/ppermute | solution.py:449
  49.2 2.8 %collective-permute-start.14 = (bf16[272,128]{1,0:T(8,128)(2,1)S(1)}, bf16[272,128]{1,0:T(8,128)(2,1)S(1)}, u32[]{:S(2)}, u32[]{:S(2)}) collective-permute-start(bf16[272,128]{1,0:T(8,128)(2,1)S(1)} %get-tuple-element.99.own), channel_id=1, source_target_pairs={{0,192},{1,193},{2,194},{3,195},{4,196},{5,197},{6,198},{7,199},{8... | collective-permute-start | bytes 208904 | tf_op jit(solution)/shard_map/ppermute | solution.py:454
  53.8 2.8 %turn.2 = (f32[2048,128]{1,0:T(8,128)S(1)}, f32[2048,128]{1,0:T(8,128)S(1)}, f32[2048,128]{1,0:T(8,128)S(1)}, f32[1024,128]{1,0:T(8,128)S(1)}, bf16[272,128]{1,0:T(8,128)(2,1)S(1)}, /*index=5*/f32[8,128]{1,0:T(8,128)S(1)}) custom-call(bf16[272,128]{1,0:T(8,128)(2,1)S(1)} %get-tuple-element.99.own, bf16[272,128]{1,0:T(8,128)(2,1)S(1)} %collective-permute-done.14.got, ...), custom_call_target="tpu_custom_call" | custom-call | tf_op jit(solution)/shard_map/turn/pallas_call | solution.py:86
  56.6 3.7 %collective-permute-start.15 = (bf16[272,128]{1,0:T(8,128)(2,1)S(1)}, bf16[272,128]{1,0:T(8,128)(2,1)S(1)}, u32[]{:S(2)}, u32[]{:S(2)}) collective-permute-start(bf16[272,128]{1,0:T(8,128)(2,1)S(1)} %get-tuple-element.104.own), channel_id=1, source_target_pairs={{0,1},{1,0},{2,3},{3,2},{4,5},{5,4},{6,7},{7,6},{8,9},{9,8},{10,11... | collective-permute-start | bytes 208904 | tf_op jit(solution)/shard_map/ppermute | solution.py:449
  62.8 2.0 %collective-permute-done.16.got = bf16[272,128]{1,0:T(8,128)(2,1)S(1)} collective-permute-done((bf16[272,128]{1,0:T(8,128)(2,1)S(1)}, bf16[272,128]{1,0:T(8,128)(2,1)S(1)}, u32[]{:S(2)}, u32[]{:S(2)}) %collective-permute-start.16) | collective-permute-done | bytes 69664 | tf_op jit(solution)/shard_map/ppermute | solution.py:449
  65.0 2.3 %collective-permute-start.17 = (bf16[272,128]{1,0:T(8,128)(2,1)S(1)}, bf16[272,128]{1,0:T(8,128)(2,1)S(1)}, u32[]{:S(2)}, u32[]{:S(2)}) collective-permute-start(bf16[272,128]{1,0:T(8,128)(2,1)S(1)} %get-tuple-element.107.own), channel_id=1, source_target_pairs={{0,4},{1,5},{2,6},{3,7},{4,0},{5,1},{6,2},{7,3},{8,12},{9,13},{10,... | collective-permute-start | bytes 208904 | tf_op jit(solution)/shard_map/ppermute | solution.py:449
  69.5 4.5 %collective-permute-start.18 = (bf16[272,128]{1,0:T(8,128)(2,1)S(1)}, bf16[272,128]{1,0:T(8,128)(2,1)S(1)}, u32[]{:S(2)}, u32[]{:S(2)}) collective-permute-start(bf16[272,128]{1,0:T(8,128)(2,1)S(1)} %get-tuple-element.109.own), channel_id=1, source_target_pairs={{0,12},{1,13},{2,14},{3,15},{4,8},{5,9},{6,10},{7,11},{8,4},{9,5},... | collective-permute-start | bytes 208904 | tf_op jit(solution)/shard_map/ppermute | solution.py:449
  76.1 3.1 %collective-permute-done.19.got = bf16[272,128]{1,0:T(8,128)(2,1)S(1)} collective-permute-done((bf16[272,128]{1,0:T(8,128)(2,1)S(1)}, bf16[272,128]{1,0:T(8,128)(2,1)S(1)}, u32[]{:S(2)}, u32[]{:S(2)}) %collective-permute-start.19) | collective-permute-done | bytes 69664 | tf_op jit(solution)/shard_map/ppermute | solution.py:449
  79.6 2.6 %collective-permute-start.20 = (bf16[272,128]{1,0:T(8,128)(2,1)S(1)}, bf16[272,128]{1,0:T(8,128)(2,1)S(1)}, u32[]{:S(2)}, u32[]{:S(2)}) collective-permute-start(bf16[272,128]{1,0:T(8,128)(2,1)S(1)} %get-tuple-element.113.own), channel_id=1, source_target_pairs={{0,48},{1,49},{2,50},{3,51},{4,52},{5,53},{6,54},{7,55},{8,56},{9,... | collective-permute-start | bytes 208904 | tf_op jit(solution)/shard_map/ppermute | solution.py:449
  82.1 1.9 %collective-permute-done.20.got = bf16[272,128]{1,0:T(8,128)(2,1)S(1)} collective-permute-done((bf16[272,128]{1,0:T(8,128)(2,1)S(1)}, bf16[272,128]{1,0:T(8,128)(2,1)S(1)}, u32[]{:S(2)}, u32[]{:S(2)}) %collective-permute-start.20) | collective-permute-done | bytes 69664 | tf_op jit(solution)/shard_map/ppermute | solution.py:449
  84.5 3.1 %collective-permute-done.21.got = bf16[272,128]{1,0:T(8,128)(2,1)S(1)} collective-permute-done((bf16[272,128]{1,0:T(8,128)(2,1)S(1)}, bf16[272,128]{1,0:T(8,128)(2,1)S(1)}, u32[]{:S(2)}, u32[]{:S(2)}) %collective-permute-start.21) | collective-permute-done | bytes 69664 | tf_op jit(solution)/shard_map/ppermute | solution.py:449
  87.9 3.0 %collective-permute-start.22 = (bf16[272,128]{1,0:T(8,128)(2,1)S(1)}, bf16[272,128]{1,0:T(8,128)(2,1)S(1)}, u32[]{:S(2)}, u32[]{:S(2)}) collective-permute-start(bf16[272,128]{1,0:T(8,128)(2,1)S(1)} %get-tuple-element.117.own), channel_id=1, source_target_pairs={{0,192},{1,193},{2,194},{3,195},{4,196},{5,197},{6,198},{7,199},{8... | collective-permute-start | bytes 208904 | tf_op jit(solution)/shard_map/ppermute | solution.py:454
  92.6 2.9 %turn.3 = (f32[2048,128]{1,0:T(8,128)S(1)}, f32[2048,128]{1,0:T(8,128)S(1)}, f32[2048,128]{1,0:T(8,128)S(1)}, f32[2048,128]{1,0:T(8,128)S(1)}, f32[1024,128]{1,0...) custom-call(bf16[272,128]{1,0:T(8,128)(2,1)S(1)} %get-tuple-element.117.own, ...), custom_call_target="tpu_custom_call" | custom-call | tf_op jit(solution)/shard_map/turn/pallas_call | solution.py:86
  95.5 8.1 %collective-permute-start.23 = (bf16[272,128]{1,0:T(8,128)(2,1)S(1)}, bf16[272,128]{1,0:T(8,128)(2,1)S(1)}, u32[]{:S(2)}, u32[]{:S(2)}) collective-permute-start(bf16[272,128]{1,0:T(8,128)(2,1)S(1)} %get-tuple-element.124.own), channel_id=1, source_target_pairs={{0,1},{1,0},{2,3},{3,2},{4,5},{5,4},{6,7},{7,6},{8,9},{9,8},{10,11... | collective-permute-start | bytes 208904 | tf_op jit(solution)/shard_map/ppermute | solution.py:449
  108.3 2.3 %collective-permute-start.25 = (bf16[272,128]{1,0:T(8,128)(2,1)S(1)}, bf16[272,128]{1,0:T(8,128)(2,1)S(1)}, u32[]{:S(2)}, u32[]{:S(2)}) collective-permute-start(bf16[272,128]{1,0:T(8,128)(2,1)S(1)} %get-tuple-element.127.own), channel_id=1, source_target_pairs={{0,4},{1,5},{2,6},{3,7},{4,0},{5,1},{6,2},{7,3},{8,12},{9,13},{10,... | collective-permute-start | bytes 208904 | tf_op jit(solution)/shard_map/ppermute | solution.py:449
  112.8 4.5 %collective-permute-start.26 = (bf16[272,128]{1,0:T(8,128)(2,1)S(1)}, bf16[272,128]{1,0:T(8,128)(2,1)S(1)}, u32[]{:S(2)}, u32[]{:S(2)}) collective-permute-start(bf16[272,128]{1,0:T(8,128)(2,1)S(1)} %get-tuple-element.129.own), channel_id=1, source_target_pairs={{0,12},{1,13},{2,14},{3,15},{4,8},{5,9},{6,10},{7,11},{8,4},{9,5},... | collective-permute-start | bytes 208904 | tf_op jit(solution)/shard_map/ppermute | solution.py:449
  119.4 3.1 %collective-permute-done.27.got = bf16[272,128]{1,0:T(8,128)(2,1)S(1)} collective-permute-done((bf16[272,128]{1,0:T(8,128)(2,1)S(1)}, bf16[272,128]{1,0:T(8,128)(2,1)S(1)}, u32[]{:S(2)}, u32[]{:S(2)}) %collective-permute-start.27) | collective-permute-done | bytes 69664 | tf_op jit(solution)/shard_map/ppermute | solution.py:449
  122.8 2.6 %collective-permute-start.28 = (bf16[272,128]{1,0:T(8,128)(2,1)S(1)}, bf16[272,128]{1,0:T(8,128)(2,1)S(1)}, u32[]{:S(2)}, u32[]{:S(2)}) collective-permute-start(bf16[272,128]{1,0:T(8,128)(2,1)S(1)} %get-tuple-element.133.own), channel_id=1, source_target_pairs={{0,48},{1,49},{2,50},{3,51},{4,52},{5,53},{6,54},{7,55},{8,56},{9,... | collective-permute-start | bytes 208904 | tf_op jit(solution)/shard_map/ppermute | solution.py:449
  125.4 1.9 %collective-permute-done.28.got = bf16[272,128]{1,0:T(8,128)(2,1)S(1)} collective-permute-done((bf16[272,128]{1,0:T(8,128)(2,1)S(1)}, bf16[272,128]{1,0:T(8,128)(2,1)S(1)}, u32[]{:S(2)}, u32[]{:S(2)}) %collective-permute-start.28) | collective-permute-done | bytes 69664 | tf_op jit(solution)/shard_map/ppermute | solution.py:449
  127.7 3.1 %collective-permute-done.29.got = bf16[272,128]{1,0:T(8,128)(2,1)S(1)} collective-permute-done((bf16[272,128]{1,0:T(8,128)(2,1)S(1)}, bf16[272,128]{1,0:T(8,128)(2,1)S(1)}, u32[]{:S(2)}, u32[]{:S(2)}) %collective-permute-start.29) | collective-permute-done | bytes 69664 | tf_op jit(solution)/shard_map/ppermute | solution.py:449
  131.1 2.8 %collective-permute-start.30 = (bf16[272,128]{1,0:T(8,128)(2,1)S(1)}, bf16[272,128]{1,0:T(8,128)(2,1)S(1)}, u32[]{:S(2)}, u32[]{:S(2)}) collective-permute-start(bf16[272,128]{1,0:T(8,128)(2,1)S(1)} %get-tuple-element.137.own), channel_id=1, source_target_pairs={{0,192},{1,193},{2,194},{3,195},{4,196},{5,197},{6,198},{7,199},{8... | collective-permute-start | bytes 208904 | tf_op jit(solution)/shard_map/ppermute | solution.py:454
  135.7 2.3 %end.1 = (f32[2048,128]{1,0:T(8,128)}, f32[2048,128]{1,0:T(8,128)S(1)}, f32[2048,128]{1,0:T(8,128)S(1)}, f32[2048,128]{1,0:T(8,128)}, f32[8,128]{1,0:T(8,128)S(1)}, /*index=5*/f32[128,128]{1,0:T(8,128)S(1)}) custom-call(bf16[272,128]{1,0:T(8,128)(2,1)S(1)} %get-tuple-element.137.own, bf16[272,128]{1,0:T(8,128)(2,1)S(1)} %collective-permute-done.30.got, ...), custom_call_target="tpu_custom_call" | custom-call | tf_op jit(solution)/shard_map/end/pallas_call | solution.py:86
  138.0 8.0 %collective-permute-start.31 = (f32[1,128]{1,0:T(1,128)S(1)}, f32[1,128]{1,0:T(1,128)S(1)}, u32[]{:S(2)}, u32[]{:S(2)}) collective-permute-start(f32[1,128]{1,0:T(1,128)S(1)} %slice.11), channel_id=1, source_target_pairs={{0,1},{1,0},{2,3},{3,2},{4,5},{5,4},{6,7},{7,6},{8,9},{9,8},{10,11... | collective-permute-start | bytes 1544 | tf_op jit(solution)/shard_map/ppermute | solution.py:466
  146.8 23.2 %all_to_all.11 = f32[128,1,128]{2,1,0:T(1,128)S(1)} all-to-all(f32[128,1,128]{2,1,0:T(1,128)S(1)} %bitcast.10), channel_id=1, replica_groups={{0,2,4,6,8,10,12,14,16,18,20,22,24,26,28,30,32,34,36,38,40,42,44,46,48,..., dimensions={0} | all-to-all | bytes 131072 | tf_op jit(solution)/shard_map/all_to_all | solution.py:468
  (88 shorter events, 45.1 us)
Async XLA Ops:
  7.1 6.4 %collective-permute-start.1 = (bf16[256,256]{1,0:T(8,128)(2,1)S(1)}, bf16[256,256]{1,0:T(8,128)(2,1)S(1)}, u32[]{:S(2)}, u32[]{:S(2)}) collective-permute-start(bf16[256,256]{1,0:T(8,128)(2,1)S(1)} %get-tuple-element.80.step), channel_id=1, source_target_pairs={{0,1},{1,0},{2,3},{3,2},{4,5},{5,4},{6,7},{7,6},{8,9},{9,8},{10,11... | collective-permute-start | bytes 393224 | tf_op jit(solution)/shard_map/ppermute | solution.py:440
  12.2 1.3 collective-permute-start
  12.6 5.2 %collective-permute-start.3 = (bf16[256,256]{1,0:T(8,128)(2,1)S(1)}, bf16[256,256]{1,0:T(8,128)(2,1)S(1)}, u32[]{:S(2)}, u32[]{:S(2)}) collective-permute-start(bf16[256,256]{1,0:T(8,128)(2,1)S(1)} %get-tuple-element.82.step), channel_id=1, source_target_pairs={{0,2},{1,3},{2,0},{3,1},{4,6},{5,7},{6,4},{7,5},{8,10},{9,11},{10,... | collective-permute-start | bytes 393224 | tf_op jit(solution)/shard_map/ppermute | solution.py:440
  13.8 7.9 %collective-permute-start.2 = (bf16[272,128]{1,0:T(8,128)(2,1)S(1)}, bf16[272,128]{1,0:T(8,128)(2,1)S(1)}, u32[]{:S(2)}, u32[]{:S(2)}) collective-permute-start(bf16[272,128]{1,0:T(8,128)(2,1)S(1)} %get-tuple-element.81.own), channel_id=1, source_target_pairs={{0,2},{1,3},{2,0},{3,1},{4,6},{5,7},{6,4},{7,5},{8,10},{9,11},{10,... | collective-permute-start | bytes 208904 | tf_op jit(solution)/shard_map/ppermute | solution.py:449
  14.4 12.7 %collective-permute-start.5 = (bf16[256,256]{1,0:T(8,128)(2,1)S(1)}, bf16[256,256]{1,0:T(8,128)(2,1)S(1)}, u32[]{:S(2)}, u32[]{:S(2)}) collective-permute-start(bf16[256,256]{1,0:T(8,128)(2,1)S(1)} %get-tuple-element.85.step), channel_id=1, source_target_pairs={{0,4},{1,5},{2,6},{3,7},{4,0},{5,1},{6,2},{7,3},{8,12},{9,13},{10,... | collective-permute-start | bytes 393224 | tf_op jit(solution)/shard_map/ppermute | solution.py:440
  22.0 5.1 %collective-permute-start.4 = (bf16[272,128]{1,0:T(8,128)(2,1)S(1)}, bf16[272,128]{1,0:T(8,128)(2,1)S(1)}, u32[]{:S(2)}, u32[]{:S(2)}) collective-permute-start(bf16[272,128]{1,0:T(8,128)(2,1)S(1)} %get-tuple-element.84.own), channel_id=1, source_target_pairs={{0,4},{1,5},{2,6},{3,7},{4,0},{5,1},{6,2},{7,3},{8,12},{9,13},{10,... | collective-permute-start | bytes 208904 | tf_op jit(solution)/shard_map/ppermute | solution.py:449
  22.1 10.3 %collective-permute-start.7 = (bf16[256,256]{1,0:T(8,128)(2,1)S(1)}, bf16[256,256]{1,0:T(8,128)(2,1)S(1)}, u32[]{:S(2)}, u32[]{:S(2)}) collective-permute-start(bf16[256,256]{1,0:T(8,128)(2,1)S(1)} %get-tuple-element.88.step), channel_id=1, source_target_pairs={{0,12},{1,13},{2,14},{3,15},{4,8},{5,9},{6,10},{7,11},{8,4},{9,5},... | collective-permute-start | bytes 393224 | tf_op jit(solution)/shard_map/ppermute | solution.py:440
  27.4 7.9 %collective-permute-start.6 = (bf16[272,128]{1,0:T(8,128)(2,1)S(1)}, bf16[272,128]{1,0:T(8,128)(2,1)S(1)}, u32[]{:S(2)}, u32[]{:S(2)}) collective-permute-start(bf16[272,128]{1,0:T(8,128)(2,1)S(1)} %get-tuple-element.87.own), channel_id=1, source_target_pairs={{0,12},{1,13},{2,14},{3,15},{4,8},{5,9},{6,10},{7,11},{8,4},{9,5},... | collective-permute-start | bytes 208904 | tf_op jit(solution)/shard_map/ppermute | solution.py:449
  29.2 9.8 %collective-permute-start.9 = (bf16[256,256]{1,0:T(8,128)(2,1)S(1)}, bf16[256,256]{1,0:T(8,128)(2,1)S(1)}, u32[]{:S(2)}, u32[]{:S(2)}) collective-permute-start(bf16[256,256]{1,0:T(8,128)(2,1)S(1)} %get-tuple-element.91.step), channel_id=1, source_target_pairs={{0,16},{1,17},{2,18},{3,19},{4,20},{5,21},{6,22},{7,23},{8,24},{9,... | collective-permute-start | bytes 393224 | tf_op jit(solution)/shard_map/ppermute | solution.py:440
  35.6 3.4 %collective-permute-start.8 = (bf16[272,128]{1,0:T(8,128)(2,1)S(1)}, bf16[272,128]{1,0:T(8,128)(2,1)S(1)}, u32[]{:S(2)}, u32[]{:S(2)}) collective-permute-start(bf16[272,128]{1,0:T(8,128)(2,1)S(1)} %get-tuple-element.90.own), channel_id=1, source_target_pairs={{0,16},{1,17},{2,18},{3,19},{4,20},{5,21},{6,22},{7,23},{8,24},{9,... | collective-permute-start | bytes 208904 | tf_op jit(solution)/shard_map/ppermute | solution.py:449
  37.1 6.1 %collective-permute-start.11 = (bf16[256,256]{1,0:T(8,128)(2,1)S(1)}, bf16[256,256]{1,0:T(8,128)(2,1)S(1)}, u32[]{:S(2)}, u32[]{:S(2)}) collective-permute-start(bf16[256,256]{1,0:T(8,128)(2,1)S(1)} %get-tuple-element.94.step), channel_id=1, source_target_pairs={{0,48},{1,49},{2,50},{3,51},{4,52},{5,53},{6,54},{7,55},{8,56},{9,... | collective-permute-start | bytes 393224 | tf_op jit(solution)/shard_map/ppermute | solution.py:440
  39.4 4.9 %collective-permute-start.10 = (bf16[272,128]{1,0:T(8,128)(2,1)S(1)}, bf16[272,128]{1,0:T(8,128)(2,1)S(1)}, u32[]{:S(2)}, u32[]{:S(2)}) collective-permute-start(bf16[272,128]{1,0:T(8,128)(2,1)S(1)} %get-tuple-element.93.own), channel_id=1, source_target_pairs={{0,48},{1,49},{2,50},{3,51},{4,52},{5,53},{6,54},{7,55},{8,56},{9,... | collective-permute-start | bytes 208904 | tf_op jit(solution)/shard_map/ppermute | solution.py:449
  41.9 4.1 %collective-permute-start.13 = (bf16[256,256]{1,0:T(8,128)(2,1)S(1)}, bf16[256,256]{1,0:T(8,128)(2,1)S(1)}, u32[]{:S(2)}, u32[]{:S(2)}) collective-permute-start(bf16[256,256]{1,0:T(8,128)(2,1)S(1)} %get-tuple-element.97.step), channel_id=1, source_target_pairs={{0,64},{1,65},{2,66},{3,67},{4,68},{5,69},{6,70},{7,71},{8,72},{9,... | collective-permute-start | bytes 393224 | tf_op jit(solution)/shard_map/ppermute | solution.py:440
  44.6 4.3 %collective-permute-start.12 = (bf16[272,128]{1,0:T(8,128)(2,1)S(1)}, bf16[272,128]{1,0:T(8,128)(2,1)S(1)}, u32[]{:S(2)}, u32[]{:S(2)}) collective-permute-start(bf16[272,128]{1,0:T(8,128)(2,1)S(1)} %get-tuple-element.96.own), channel_id=1, source_target_pairs={{0,64},{1,65},{2,66},{3,67},{4,68},{5,69},{6,70},{7,71},{8,72},{9,... | collective-permute-start | bytes 208904 | tf_op jit(solution)/shard_map/ppermute | solution.py:449
  49.2 4.5 %collective-permute-start.14 = (bf16[272,128]{1,0:T(8,128)(2,1)S(1)}, bf16[272,128]{1,0:T(8,128)(2,1)S(1)}, u32[]{:S(2)}, u32[]{:S(2)}) collective-permute-start(bf16[272,128]{1,0:T(8,128)(2,1)S(1)} %get-tuple-element.99.own), channel_id=1, source_target_pairs={{0,192},{1,193},{2,194},{3,195},{4,196},{5,197},{6,198},{7,199},{8... | collective-permute-start | bytes 208904 | tf_op jit(solution)/shard_map/ppermute | solution.py:454
  56.6 4.6 %collective-permute-start.15 = (bf16[272,128]{1,0:T(8,128)(2,1)S(1)}, bf16[272,128]{1,0:T(8,128)(2,1)S(1)}, u32[]{:S(2)}, u32[]{:S(2)}) collective-permute-start(bf16[272,128]{1,0:T(8,128)(2,1)S(1)} %get-tuple-element.104.own), channel_id=1, source_target_pairs={{0,1},{1,0},{2,3},{3,2},{4,5},{5,4},{6,7},{7,6},{8,9},{9,8},{10,11... | collective-permute-start | bytes 208904 | tf_op jit(solution)/shard_map/ppermute | solution.py:449
  61.5 3.2 %collective-permute-start.16 = (bf16[272,128]{1,0:T(8,128)(2,1)S(1)}, bf16[272,128]{1,0:T(8,128)(2,1)S(1)}, u32[]{:S(2)}, u32[]{:S(2)}) collective-permute-start(bf16[272,128]{1,0:T(8,128)(2,1)S(1)} %get-tuple-element.105.own), channel_id=1, source_target_pairs={{0,2},{1,3},{2,0},{3,1},{4,6},{5,7},{6,4},{7,5},{8,10},{9,11},{10,... | collective-permute-start | bytes 208904 | tf_op jit(solution)/shard_map/ppermute | solution.py:449
  65.0 4.1 %collective-permute-start.17 = (bf16[272,128]{1,0:T(8,128)(2,1)S(1)}, bf16[272,128]{1,0:T(8,128)(2,1)S(1)}, u32[]{:S(2)}, u32[]{:S(2)}) collective-permute-start(bf16[272,128]{1,0:T(8,128)(2,1)S(1)} %get-tuple-element.107.own), channel_id=1, source_target_pairs={{0,4},{1,5},{2,6},{3,7},{4,0},{5,1},{6,2},{7,3},{8,12},{9,13},{10,... | collective-permute-start | bytes 208904 | tf_op jit(solution)/shard_map/ppermute | solution.py:449
  69.5 6.2 %collective-permute-start.18 = (bf16[272,128]{1,0:T(8,128)(2,1)S(1)}, bf16[272,128]{1,0:T(8,128)(2,1)S(1)}, u32[]{:S(2)}, u32[]{:S(2)}) collective-permute-start(bf16[272,128]{1,0:T(8,128)(2,1)S(1)} %get-tuple-element.109.own), channel_id=1, source_target_pairs={{0,12},{1,13},{2,14},{3,15},{4,8},{5,9},{6,10},{7,11},{8,4},{9,5},... | collective-permute-start | bytes 208904 | tf_op jit(solution)/shard_map/ppermute | solution.py:449
  76.0 3.2 %collective-permute-start.19 = (bf16[272,128]{1,0:T(8,128)(2,1)S(1)}, bf16[272,128]{1,0:T(8,128)(2,1)S(1)}, u32[]{:S(2)}, u32[]{:S(2)}) collective-permute-start(bf16[272,128]{1,0:T(8,128)(2,1)S(1)} %get-tuple-element.111.own), channel_id=1, source_target_pairs={{0,16},{1,17},{2,18},{3,19},{4,20},{5,21},{6,22},{7,23},{8,24},{9,... | collective-permute-start | bytes 208904 | tf_op jit(solution)/shard_map/ppermute | solution.py:449
  79.6 4.5 %collective-permute-start.20 = (bf16[272,128]{1,0:T(8,128)(2,1)S(1)}, bf16[272,128]{1,0:T(8,128)(2,1)S(1)}, u32[]{:S(2)}, u32[]{:S(2)}) collective-permute-start(bf16[272,128]{1,0:T(8,128)(2,1)S(1)} %get-tuple-element.113.own), channel_id=1, source_target_pairs={{0,48},{1,49},{2,50},{3,51},{4,52},{5,53},{6,54},{7,55},{8,56},{9,... | collective-permute-start | bytes 208904 | tf_op jit(solution)/shard_map/ppermute | solution.py:449
  84.3 3.2 %collective-permute-start.21 = (bf16[272,128]{1,0:T(8,128)(2,1)S(1)}, bf16[272,128]{1,0:T(8,128)(2,1)S(1)}, u32[]{:S(2)}, u32[]{:S(2)}) collective-permute-start(bf16[272,128]{1,0:T(8,128)(2,1)S(1)} %get-tuple-element.115.own), channel_id=1, source_target_pairs={{0,64},{1,65},{2,66},{3,67},{4,68},{5,69},{6,70},{7,71},{8,72},{9,... | collective-permute-start | bytes 208904 | tf_op jit(solution)/shard_map/ppermute | solution.py:449
  87.9 4.7 %collective-permute-start.22 = (bf16[272,128]{1,0:T(8,128)(2,1)S(1)}, bf16[272,128]{1,0:T(8,128)(2,1)S(1)}, u32[]{:S(2)}, u32[]{:S(2)}) collective-permute-start(bf16[272,128]{1,0:T(8,128)(2,1)S(1)} %get-tuple-element.117.own), channel_id=1, source_target_pairs={{0,192},{1,193},{2,194},{3,195},{4,196},{5,197},{6,198},{7,199},{8... | collective-permute-start | bytes 208904 | tf_op jit(solution)/shard_map/ppermute | solution.py:454
  95.5 9.0 %collective-permute-start.23 = (bf16[272,128]{1,0:T(8,128)(2,1)S(1)}, bf16[272,128]{1,0:T(8,128)(2,1)S(1)}, u32[]{:S(2)}, u32[]{:S(2)}) collective-permute-start(bf16[272,128]{1,0:T(8,128)(2,1)S(1)} %get-tuple-element.124.own), channel_id=1, source_target_pairs={{0,1},{1,0},{2,3},{3,2},{4,5},{5,4},{6,7},{7,6},{8,9},{9,8},{10,11... | collective-permute-start | bytes 208904 | tf_op jit(solution)/shard_map/ppermute | solution.py:449
  104.8 3.2 %collective-permute-start.24 = (bf16[272,128]{1,0:T(8,128)(2,1)S(1)}, bf16[272,128]{1,0:T(8,128)(2,1)S(1)}, u32[]{:S(2)}, u32[]{:S(2)}) collective-permute-start(bf16[272,128]{1,0:T(8,128)(2,1)S(1)} %get-tuple-element.125.own), channel_id=1, source_target_pairs={{0,2},{1,3},{2,0},{3,1},{4,6},{5,7},{6,4},{7,5},{8,10},{9,11},{10,... | collective-permute-start | bytes 208904 | tf_op jit(solution)/shard_map/ppermute | solution.py:449
  108.3 4.1 %collective-permute-start.25 = (bf16[272,128]{1,0:T(8,128)(2,1)S(1)}, bf16[272,128]{1,0:T(8,128)(2,1)S(1)}, u32[]{:S(2)}, u32[]{:S(2)}) collective-permute-start(bf16[272,128]{1,0:T(8,128)(2,1)S(1)} %get-tuple-element.127.own), channel_id=1, source_target_pairs={{0,4},{1,5},{2,6},{3,7},{4,0},{5,1},{6,2},{7,3},{8,12},{9,13},{10,... | collective-permute-start | bytes 208904 | tf_op jit(solution)/shard_map/ppermute | solution.py:449
  112.8 6.2 %collective-permute-start.26 = (bf16[272,128]{1,0:T(8,128)(2,1)S(1)}, bf16[272,128]{1,0:T(8,128)(2,1)S(1)}, u32[]{:S(2)}, u32[]{:S(2)}) collective-permute-start(bf16[272,128]{1,0:T(8,128)(2,1)S(1)} %get-tuple-element.129.own), channel_id=1, source_target_pairs={{0,12},{1,13},{2,14},{3,15},{4,8},{5,9},{6,10},{7,11},{8,4},{9,5},... | collective-permute-start | bytes 208904 | tf_op jit(solution)/shard_map/ppermute | solution.py:449
  119.3 3.2 %collective-permute-start.27 = (bf16[272,128]{1,0:T(8,128)(2,1)S(1)}, bf16[272,128]{1,0:T(8,128)(2,1)S(1)}, u32[]{:S(2)}, u32[]{:S(2)}) collective-permute-start(bf16[272,128]{1,0:T(8,128)(2,1)S(1)} %get-tuple-element.131.own), channel_id=1, source_target_pairs={{0,16},{1,17},{2,18},{3,19},{4,20},{5,21},{6,22},{7,23},{8,24},{9,... | collective-permute-start | bytes 208904 | tf_op jit(solution)/shard_map/ppermute | solution.py:449
  122.8 4.5 %collective-permute-start.28 = (bf16[272,128]{1,0:T(8,128)(2,1)S(1)}, bf16[272,128]{1,0:T(8,128)(2,1)S(1)}, u32[]{:S(2)}, u32[]{:S(2)}) collective-permute-start(bf16[272,128]{1,0:T(8,128)(2,1)S(1)} %get-tuple-element.133.own), channel_id=1, source_target_pairs={{0,48},{1,49},{2,50},{3,51},{4,52},{5,53},{6,54},{7,55},{8,56},{9,... | collective-permute-start | bytes 208904 | tf_op jit(solution)/shard_map/ppermute | solution.py:449
  127.6 3.2 %collective-permute-start.29 = (bf16[272,128]{1,0:T(8,128)(2,1)S(1)}, bf16[272,128]{1,0:T(8,128)(2,1)S(1)}, u32[]{:S(2)}, u32[]{:S(2)}) collective-permute-start(bf16[272,128]{1,0:T(8,128)(2,1)S(1)} %get-tuple-element.135.own), channel_id=1, source_target_pairs={{0,64},{1,65},{2,66},{3,67},{4,68},{5,69},{6,70},{7,71},{8,72},{9,... | collective-permute-start | bytes 208904 | tf_op jit(solution)/shard_map/ppermute | solution.py:449
  131.1 4.5 %collective-permute-start.30 = (bf16[272,128]{1,0:T(8,128)(2,1)S(1)}, bf16[272,128]{1,0:T(8,128)(2,1)S(1)}, u32[]{:S(2)}, u32[]{:S(2)}) collective-permute-start(bf16[272,128]{1,0:T(8,128)(2,1)S(1)} %get-tuple-element.137.own), channel_id=1, source_target_pairs={{0,192},{1,193},{2,194},{3,195},{4,196},{5,197},{6,198},{7,199},{8... | collective-permute-start | bytes 208904 | tf_op jit(solution)/shard_map/ppermute | solution.py:454
  138.0 8.8 %collective-permute-start.31 = (f32[1,128]{1,0:T(1,128)S(1)}, f32[1,128]{1,0:T(1,128)S(1)}, u32[]{:S(2)}, u32[]{:S(2)}) collective-permute-start(f32[1,128]{1,0:T(1,128)S(1)} %slice.11), channel_id=1, source_target_pairs={{0,1},{1,0},{2,3},{3,2},{4,5},{5,4},{6,7},{7,6},{8,9},{9,8},{10,11... | collective-permute-start | bytes 1544 | tf_op jit(solution)/shard_map/ppermute | solution.py:466
  (10 other events, 41.6 us)

commit v3 on v1

--- a/solution.py
+++ b/solution.py
@@ -109,11 +109,22 @@
     for piece in split3(value):
         pieces += [piece.astype(F32), gap]
     pieces = jnp.concatenate(pieces, axis=0).astype(BF)
-    place = lax.broadcasted_iota(jnp.int32, (total, ROWS), 0)
+    lanes = 128
+    blocks = total // lanes
+    height = pieces.shape[0]
+    stacked = jnp.concatenate(
+        [pieces[:, c * lanes : (c + 1) * lanes] for c in range(blocks)], axis=0
+    )
+    place = lax.broadcasted_iota(jnp.int32, (lanes, ROWS), 0)
     for i in range(LEAVES):
         picked = order_ref[:, i * ROWS : (i + 1) * ROWS]
-        chosen = jnp.where(place == picked, 1.0, 0.0).astype(BF)
-        moved = dot(pieces, chosen)
+        chosen = jnp.where(place == (picked & (lanes - 1)), 1.0, 0.0).astype(BF)
+        found = dot(stacked, chosen)
+        block = picked >> 7
+        moved = jnp.zeros((height, ROWS), F32)
+        for c in range(blocks):
+            part = found[c * height : (c + 1) * height]
+            moved = moved + part * jnp.where(block == c, 1.0, 0.0)
         high, mid, low = moved[0:32], moved[32:64], moved[64:96]
         full = high + mid + low
         half = -0.5 * jnp.sum(full * full, axis=0, keepdims=True)

time: 170 us -> 170 us (level)
  no operation moved by 1% of the time
where the time goes in v3:
time: 170 us
  starting transfers between devices  69.6 us (41%)
  waiting for transfers between devices  51.8 us (30%)
  blocking collectives  23.3 us (14%)
  Pallas kernels  22.4 us (13%)
  local copies, waits for them, and re-layouts  1.84 us (1%)
    ppermute x21, waiting for transfers between devices, per_device(): got = lax.ppermute(payload, 'leaf', routes[level])  45.2 us
    ppermute x21, starting transfers between devices, per_device(): got = lax.ppermute(payload, 'leaf', routes[level])  41 us
    all_to_all x1, blocking collectives, per_device(): lax.all_to_all(chip, 'leaf', 0, 0, axis_index_groups=same_core, tiled=True)  23.3 us
    ppermute x7, starting transfers between devices, per_device(): lax.ppermute(block, 'leaf', route)  13.5 us
    pallas_call x6, Pallas kernels, call(): pl.pallas_call(kernel, in_specs=[in_vmem] * len(operands), out_specs=[in_...  11.7 us
    ppermute x3, starting transfers between devices, per_device(): got = lax.ppermute(payload, 'leaf', routes[LEVELS - 1])  8.04 us
    ppermute x1, starting transfers between devices, per_device(): chip = sums + lax.ppermute(sums[0:1], 'leaf', routes[0])  6.95 us
    pallas_call x21, Pallas kernels, climb(): pl.pallas_call(functools.partial(climb_kernel, level), in_specs=[in_vmem]...  6.3 us
  transfers between devices with their start and end apart: 32, of which 25 were waited for; matrix products, arithmetic and copies ran while one was open for 0% of the time, Pallas kernels for 3%

profile of v3, /device:TPU:1, one launch (start us, length us, event | category | flops | bytes accessed | tf_op | source)
XLA Modules:
  0.0 170.0 jit_solution(13513671679337434362)
XLA Ops:
  2.5 3.2 %leaf_kernels.1._.kernel.rest_6_.rest_7_ = bf16[4,512,512]{2,1,0:T(8,128)(2,1)S(1)} custom-call(f32[28,2048]{1,0:T(8,128)S(1)} %copy-done.7, s32[1,2048]{1,0:T(1,128)S(1)} %copy-done.8), custom_call_target="tpu_custom_call" | custom-call | flops 1241513984 | bytes 4194304 | tf_op jit(solution)/shard_map/leaf_kernels/pallas_call | solution.py:148
  6.9 3.3 %collective-permute-start.1 = (bf16[256,256]{1,0:T(8,128)(2,1)S(1)}, bf16[256,256]{1,0:T(8,128)(2,1)S(1)}, u32[]{:S(2)}, u32[]{:S(2)}) collective-permute-start(bf16[256,256]{1,0:T(8,128)(2,1)S(1)} %get-tuple-element.80.step), channel_id=1, source_target_pairs={{0,1},{1,0},{2,3},{3,2},{4,5},{5,4},{6,7},{7,6},{8,9},{9,8},{10,11... | collective-permute-start | bytes 393224 | tf_op jit(solution)/shard_map/ppermute | solution.py:448
  20.2 4.4 %collective-permute-start.7 = (bf16[256,256]{1,0:T(8,128)(2,1)S(1)}, bf16[256,256]{1,0:T(8,128)(2,1)S(1)}, u32[]{:S(2)}, u32[]{:S(2)}) collective-permute-start(bf16[256,256]{1,0:T(8,128)(2,1)S(1)} %get-tuple-element.88.step), channel_id=1, source_target_pairs={{0,12},{1,13},{2,14},{3,15},{4,8},{5,9},{6,10},{7,11},{8,4},{9,5},... | collective-permute-start | bytes 393224 | tf_op jit(solution)/shard_map/ppermute | solution.py:448
  29.5 2.7 %collective-permute-done.6.got = bf16[272,128]{1,0:T(8,128)(2,1)S(1)} collective-permute-done((bf16[272,128]{1,0:T(8,128)(2,1)S(1)}, bf16[272,128]{1,0:T(8,128)(2,1)S(1)}, u32[]{:S(2)}, u32[]{:S(2)}) %collective-permute-start.6) | collective-permute-done | bytes 69664 | tf_op jit(solution)/shard_map/ppermute | solution.py:457
  36.4 2.6 %collective-permute-start.10 = (bf16[272,128]{1,0:T(8,128)(2,1)S(1)}, bf16[272,128]{1,0:T(8,128)(2,1)S(1)}, u32[]{:S(2)}, u32[]{:S(2)}) collective-permute-start(bf16[272,128]{1,0:T(8,128)(2,1)S(1)} %get-tuple-element.93.own), channel_id=1, source_target_pairs={{0,48},{1,49},{2,50},{3,51},{4,52},{5,53},{6,54},{7,55},{8,56},{9,... | collective-permute-start | bytes 208904 | tf_op jit(solution)/shard_map/ppermute | solution.py:457
  43.2 2.0 %collective-permute-done.12.got = bf16[272,128]{1,0:T(8,128)(2,1)S(1)} collective-permute-done((bf16[272,128]{1,0:T(8,128)(2,1)S(1)}, bf16[272,128]{1,0:T(8,128)(2,1)S(1)}, u32[]{:S(2)}, u32[]{:S(2)}) %collective-permute-start.12) | collective-permute-done | bytes 69664 | tf_op jit(solution)/shard_map/ppermute | solution.py:457
  45.5 2.6 %collective-permute-start.14 = (bf16[272,128]{1,0:T(8,128)(2,1)S(1)}, bf16[272,128]{1,0:T(8,128)(2,1)S(1)}, u32[]{:S(2)}, u32[]{:S(2)}) collective-permute-start(bf16[272,128]{1,0:T(8,128)(2,1)S(1)} %get-tuple-element.99.own), channel_id=1, source_target_pairs={{0,192},{1,193},{2,194},{3,195},{4,196},{5,197},{6,198},{7,199},{8... | collective-permute-start | bytes 208904 | tf_op jit(solution)/shard_map/ppermute | solution.py:461
  50.0 2.8 %turn.2 = (f32[2048,128]{1,0:T(8,128)S(1)}, f32[2048,128]{1,0:T(8,128)S(1)}, f32[2048,128]{1,0:T(8,128)S(1)}, f32[1024,128]{1,0:T(8,128)S(1)}, bf16[272,128]{1,0:T(8,128)(2,1)S(1)}, /*index=5*/f32[8,128]{1,0:T(8,128)S(1)}) custom-call(bf16[272,128]{1,0:T(8,128)(2,1)S(1)} %get-tuple-element.99.own, bf16[272,128]{1,0:T(8,128)(2,1)S(1)} %collective-permute-done.14.got, ...), custom_call_target="tpu_custom_call" | custom-call | tf_op jit(solution)/shard_map/turn/pallas_call | solution.py:86
  52.8 6.3 %collective-permute-start.15 = (bf16[272,128]{1,0:T(8,128)(2,1)S(1)}, bf16[272,128]{1,0:T(8,128)(2,1)S(1)}, u32[]{:S(2)}, u32[]{:S(2)}) collective-permute-start(bf16[272,128]{1,0:T(8,128)(2,1)S(1)} %get-tuple-element.104.own), channel_id=1, source_target_pairs={{0,1},{1,0},{2,3},{3,2},{4,5},{5,4},{6,7},{7,6},{8,9},{9,8},{10,11... | collective-permute-start | bytes 208904 | tf_op jit(solution)/shard_map/ppermute | solution.py:457
  62.2 2.3 %collective-permute-done.16.got = bf16[272,128]{1,0:T(8,128)(2,1)S(1)} collective-permute-done((bf16[272,128]{1,0:T(8,128)(2,1)S(1)}, bf16[272,128]{1,0:T(8,128)(2,1)S(1)}, u32[]{:S(2)}, u32[]{:S(2)}) %collective-permute-start.16) | collective-permute-done | bytes 69664 | tf_op jit(solution)/shard_map/ppermute | solution.py:457
  66.7 3.0 %collective-permute-done.17.got = bf16[272,128]{1,0:T(8,128)(2,1)S(1)} collective-permute-done((bf16[272,128]{1,0:T(8,128)(2,1)S(1)}, bf16[272,128]{1,0:T(8,128)(2,1)S(1)}, u32[]{:S(2)}, u32[]{:S(2)}) %collective-permute-start.17) | collective-permute-done | bytes 69664 | tf_op jit(solution)/shard_map/ppermute | solution.py:457
  70.0 2.5 %collective-permute-start.18 = (bf16[272,128]{1,0:T(8,128)(2,1)S(1)}, bf16[272,128]{1,0:T(8,128)(2,1)S(1)}, u32[]{:S(2)}, u32[]{:S(2)}) collective-permute-start(bf16[272,128]{1,0:T(8,128)(2,1)S(1)} %get-tuple-element.109.own), channel_id=1, source_target_pairs={{0,12},{1,13},{2,14},{3,15},{4,8},{5,9},{6,10},{7,11},{8,4},{9,5},... | collective-permute-start | bytes 208904 | tf_op jit(solution)/shard_map/ppermute | solution.py:457
  72.5 2.8 %collective-permute-done.18.got = bf16[272,128]{1,0:T(8,128)(2,1)S(1)} collective-permute-done((bf16[272,128]{1,0:T(8,128)(2,1)S(1)}, bf16[272,128]{1,0:T(8,128)(2,1)S(1)}, u32[]{:S(2)}, u32[]{:S(2)}) %collective-permute-start.18) | collective-permute-done | bytes 69664 | tf_op jit(solution)/shard_map/ppermute | solution.py:457
  75.7 3.1 %collective-permute-done.19.got = bf16[272,128]{1,0:T(8,128)(2,1)S(1)} collective-permute-done((bf16[272,128]{1,0:T(8,128)(2,1)S(1)}, bf16[272,128]{1,0:T(8,128)(2,1)S(1)}, u32[]{:S(2)}, u32[]{:S(2)}) %collective-permute-start.19) | collective-permute-done | bytes 69664 | tf_op jit(solution)/shard_map/ppermute | solution.py:457
  79.2 2.3 %collective-permute-start.20 = (bf16[272,128]{1,0:T(8,128)(2,1)S(1)}, bf16[272,128]{1,0:T(8,128)(2,1)S(1)}, u32[]{:S(2)}, u32[]{:S(2)}) collective-permute-start(bf16[272,128]{1,0:T(8,128)(2,1)S(1)} %get-tuple-element.113.own), channel_id=1, source_target_pairs={{0,48},{1,49},{2,50},{3,51},{4,52},{5,53},{6,54},{7,55},{8,56},{9,... | collective-permute-start | bytes 208904 | tf_op jit(solution)/shard_map/ppermute | solution.py:457
  81.5 2.2 %collective-permute-done.20.got = bf16[272,128]{1,0:T(8,128)(2,1)S(1)} collective-permute-done((bf16[272,128]{1,0:T(8,128)(2,1)S(1)}, bf16[272,128]{1,0:T(8,128)(2,1)S(1)}, u32[]{:S(2)}, u32[]{:S(2)}) %collective-permute-start.20) | collective-permute-done | bytes 69664 | tf_op jit(solution)/shard_map/ppermute | solution.py:457
  84.0 3.4 %collective-permute-done.21.got = bf16[272,128]{1,0:T(8,128)(2,1)S(1)} collective-permute-done((bf16[272,128]{1,0:T(8,128)(2,1)S(1)}, bf16[272,128]{1,0:T(8,128)(2,1)S(1)}, u32[]{:S(2)}, u32[]{:S(2)}) %collective-permute-start.21) | collective-permute-done | bytes 69664 | tf_op jit(solution)/shard_map/ppermute | solution.py:457
  87.8 2.8 %collective-permute-start.22 = (bf16[272,128]{1,0:T(8,128)(2,1)S(1)}, bf16[272,128]{1,0:T(8,128)(2,1)S(1)}, u32[]{:S(2)}, u32[]{:S(2)}) collective-permute-start(bf16[272,128]{1,0:T(8,128)(2,1)S(1)} %get-tuple-element.117.own), channel_id=1, source_target_pairs={{0,192},{1,193},{2,194},{3,195},{4,196},{5,197},{6,198},{7,199},{8... | collective-permute-start | bytes 208904 | tf_op jit(solution)/shard_map/ppermute | solution.py:461
  92.5 2.8 %turn.3 = (f32[2048,128]{1,0:T(8,128)S(1)}, f32[2048,128]{1,0:T(8,128)S(1)}, f32[2048,128]{1,0:T(8,128)S(1)}, f32[2048,128]{1,0:T(8,128)S(1)}, f32[1024,128]{1,0...) custom-call(bf16[272,128]{1,0:T(8,128)(2,1)S(1)} %get-tuple-element.117.own, ...), custom_call_target="tpu_custom_call" | custom-call | tf_op jit(solution)/shard_map/turn/pallas_call | solution.py:86
  95.3 7.0 %collective-permute-start.23 = (bf16[272,128]{1,0:T(8,128)(2,1)S(1)}, bf16[272,128]{1,0:T(8,128)(2,1)S(1)}, u32[]{:S(2)}, u32[]{:S(2)}) collective-permute-start(bf16[272,128]{1,0:T(8,128)(2,1)S(1)} %get-tuple-element.124.own), channel_id=1, source_target_pairs={{0,1},{1,0},{2,3},{3,2},{4,5},{5,4},{6,7},{7,6},{8,9},{9,8},{10,11... | collective-permute-start | bytes 208904 | tf_op jit(solution)/shard_map/ppermute | solution.py:457
  105.5 2.3 %collective-permute-done.24.got = bf16[272,128]{1,0:T(8,128)(2,1)S(1)} collective-permute-done((bf16[272,128]{1,0:T(8,128)(2,1)S(1)}, bf16[272,128]{1,0:T(8,128)(2,1)S(1)}, u32[]{:S(2)}, u32[]{:S(2)}) %collective-permute-start.24) | collective-permute-done | bytes 69664 | tf_op jit(solution)/shard_map/ppermute | solution.py:457
  109.8 3.1 %collective-permute-done.25.got = bf16[272,128]{1,0:T(8,128)(2,1)S(1)} collective-permute-done((bf16[272,128]{1,0:T(8,128)(2,1)S(1)}, bf16[272,128]{1,0:T(8,128)(2,1)S(1)}, u32[]{:S(2)}, u32[]{:S(2)}) %collective-permute-start.25) | collective-permute-done | bytes 69664 | tf_op jit(solution)/shard_map/ppermute | solution.py:457
  113.2 2.4 %collective-permute-start.26 = (bf16[272,128]{1,0:T(8,128)(2,1)S(1)}, bf16[272,128]{1,0:T(8,128)(2,1)S(1)}, u32[]{:S(2)}, u32[]{:S(2)}) collective-permute-start(bf16[272,128]{1,0:T(8,128)(2,1)S(1)} %get-tuple-element.129.own), channel_id=1, source_target_pairs={{0,12},{1,13},{2,14},{3,15},{4,8},{5,9},{6,10},{7,11},{8,4},{9,5},... | collective-permute-start | bytes 208904 | tf_op jit(solution)/shard_map/ppermute | solution.py:457
  115.6 3.0 %collective-permute-done.26.got = bf16[272,128]{1,0:T(8,128)(2,1)S(1)} collective-permute-done((bf16[272,128]{1,0:T(8,128)(2,1)S(1)}, bf16[272,128]{1,0:T(8,128)(2,1)S(1)}, u32[]{:S(2)}, u32[]{:S(2)}) %collective-permute-start.26) | collective-permute-done | bytes 69664 | tf_op jit(solution)/shard_map/ppermute | solution.py:457
  119.0 3.1 %collective-permute-done.27.got = bf16[272,128]{1,0:T(8,128)(2,1)S(1)} collective-permute-done((bf16[272,128]{1,0:T(8,128)(2,1)S(1)}, bf16[272,128]{1,0:T(8,128)(2,1)S(1)}, u32[]{:S(2)}, u32[]{:S(2)}) %collective-permute-start.27) | collective-permute-done | bytes 69664 | tf_op jit(solution)/shard_map/ppermute | solution.py:457
  122.4 2.4 %collective-permute-start.28 = (bf16[272,128]{1,0:T(8,128)(2,1)S(1)}, bf16[272,128]{1,0:T(8,128)(2,1)S(1)}, u32[]{:S(2)}, u32[]{:S(2)}) collective-permute-start(bf16[272,128]{1,0:T(8,128)(2,1)S(1)} %get-tuple-element.133.own), channel_id=1, source_target_pairs={{0,48},{1,49},{2,50},{3,51},{4,52},{5,53},{6,54},{7,55},{8,56},{9,... | collective-permute-start | bytes 208904 | tf_op jit(solution)/shard_map/ppermute | solution.py:457
  124.8 2.1 %collective-permute-done.28.got = bf16[272,128]{1,0:T(8,128)(2,1)S(1)} collective-permute-done((bf16[272,128]{1,0:T(8,128)(2,1)S(1)}, bf16[272,128]{1,0:T(8,128)(2,1)S(1)}, u32[]{:S(2)}, u32[]{:S(2)}) %collective-permute-start.28) | collective-permute-done | bytes 69664 | tf_op jit(solution)/shard_map/ppermute | solution.py:457
  127.3 3.4 %collective-permute-done.29.got = bf16[272,128]{1,0:T(8,128)(2,1)S(1)} collective-permute-done((bf16[272,128]{1,0:T(8,128)(2,1)S(1)}, bf16[272,128]{1,0:T(8,128)(2,1)S(1)}, u32[]{:S(2)}, u32[]{:S(2)}) %collective-permute-start.29) | collective-permute-done | bytes 69664 | tf_op jit(solution)/shard_map/ppermute | solution.py:457
  131.0 2.6 %collective-permute-start.30 = (bf16[272,128]{1,0:T(8,128)(2,1)S(1)}, bf16[272,128]{1,0:T(8,128)(2,1)S(1)}, u32[]{:S(2)}, u32[]{:S(2)}) collective-permute-start(bf16[272,128]{1,0:T(8,128)(2,1)S(1)} %get-tuple-element.137.own), channel_id=1, source_target_pairs={{0,192},{1,193},{2,194},{3,195},{4,196},{5,197},{6,198},{7,199},{8... | collective-permute-start | bytes 208904 | tf_op jit(solution)/shard_map/ppermute | solution.py:461
  135.5 2.3 %end.1 = (f32[2048,128]{1,0:T(8,128)}, f32[2048,128]{1,0:T(8,128)S(1)}, f32[2048,128]{1,0:T(8,128)S(1)}, f32[2048,128]{1,0:T(8,128)}, f32[8,128]{1,0:T(8,128)S(1)}, /*index=5*/f32[128,128]{1,0:T(8,128)S(1)}) custom-call(bf16[272,128]{1,0:T(8,128)(2,1)S(1)} %get-tuple-element.137.own, bf16[272,128]{1,0:T(8,128)(2,1)S(1)} %collective-permute-done.30.got, ...), custom_call_target="tpu_custom_call" | custom-call | tf_op jit(solution)/shard_map/end/pallas_call | solution.py:86
  137.8 6.9 %collective-permute-start.31 = (f32[1,128]{1,0:T(1,128)S(1)}, f32[1,128]{1,0:T(1,128)S(1)}, u32[]{:S(2)}, u32[]{:S(2)}) collective-permute-start(f32[1,128]{1,0:T(1,128)S(1)} %slice.11), channel_id=1, source_target_pairs={{0,1},{1,0},{2,3},{3,2},{4,5},{5,4},{6,7},{7,6},{8,9},{9,8},{10,11... | collective-permute-start | bytes 1544 | tf_op jit(solution)/shard_map/ppermute | solution.py:473
  145.6 23.3 %all_to_all.11 = f32[128,1,128]{2,1,0:T(1,128)S(1)} all-to-all(f32[128,1,128]{2,1,0:T(1,128)S(1)} %bitcast.10), channel_id=1, replica_groups={{0,2,4,6,8,10,12,14,16,18,20,22,24,26,28,30,32,34,36,38,40,42,44,46,48,..., dimensions={0} | all-to-all | bytes 131072 | tf_op jit(solution)/shard_map/all_to_all | solution.py:475
  (88 shorter events, 48.0 us)
Async XLA Ops:
  6.9 6.5 %collective-permute-start.1 = (bf16[256,256]{1,0:T(8,128)(2,1)S(1)}, bf16[256,256]{1,0:T(8,128)(2,1)S(1)}, u32[]{:S(2)}, u32[]{:S(2)}) collective-permute-start(bf16[256,256]{1,0:T(8,128)(2,1)S(1)} %get-tuple-element.80.step), channel_id=1, source_target_pairs={{0,1},{1,0},{2,3},{3,2},{4,5},{5,4},{6,7},{7,6},{8,9},{9,8},{10,11... | collective-permute-start | bytes 393224 | tf_op jit(solution)/shard_map/ppermute | solution.py:448
  12.0 1.4 collective-permute-start
  12.4 4.9 %collective-permute-start.3 = (bf16[256,256]{1,0:T(8,128)(2,1)S(1)}, bf16[256,256]{1,0:T(8,128)(2,1)S(1)}, u32[]{:S(2)}, u32[]{:S(2)}) collective-permute-start(bf16[256,256]{1,0:T(8,128)(2,1)S(1)} %get-tuple-element.82.step), channel_id=1, source_target_pairs={{0,2},{1,3},{2,0},{3,1},{4,6},{5,7},{6,4},{7,5},{8,10},{9,11},{10,... | collective-permute-start | bytes 393224 | tf_op jit(solution)/shard_map/ppermute | solution.py:448
  13.7 5.1 %collective-permute-start.2 = (bf16[272,128]{1,0:T(8,128)(2,1)S(1)}, bf16[272,128]{1,0:T(8,128)(2,1)S(1)}, u32[]{:S(2)}, u32[]{:S(2)}) collective-permute-start(bf16[272,128]{1,0:T(8,128)(2,1)S(1)} %get-tuple-element.81.own), channel_id=1, source_target_pairs={{0,2},{1,3},{2,0},{3,1},{4,6},{5,7},{6,4},{7,5},{8,10},{9,11},{10,... | collective-permute-start | bytes 208904 | tf_op jit(solution)/shard_map/ppermute | solution.py:457
  15.2 9.4 %collective-permute-start.5 = (bf16[256,256]{1,0:T(8,128)(2,1)S(1)}, bf16[256,256]{1,0:T(8,128)(2,1)S(1)}, u32[]{:S(2)}, u32[]{:S(2)}) collective-permute-start(bf16[256,256]{1,0:T(8,128)(2,1)S(1)} %get-tuple-element.85.step), channel_id=1, source_target_pairs={{0,4},{1,5},{2,6},{3,7},{4,0},{5,1},{6,2},{7,3},{8,12},{9,13},{10,... | collective-permute-start | bytes 393224 | tf_op jit(solution)/shard_map/ppermute | solution.py:448
  19.0 7.3 %collective-permute-start.4 = (bf16[272,128]{1,0:T(8,128)(2,1)S(1)}, bf16[272,128]{1,0:T(8,128)(2,1)S(1)}, u32[]{:S(2)}, u32[]{:S(2)}) collective-permute-start(bf16[272,128]{1,0:T(8,128)(2,1)S(1)} %get-tuple-element.84.own), channel_id=1, source_target_pairs={{0,4},{1,5},{2,6},{3,7},{4,0},{5,1},{6,2},{7,3},{8,12},{9,13},{10,... | collective-permute-start | bytes 208904 | tf_op jit(solution)/shard_map/ppermute | solution.py:457
  20.2 9.3 %collective-permute-start.7 = (bf16[256,256]{1,0:T(8,128)(2,1)S(1)}, bf16[256,256]{1,0:T(8,128)(2,1)S(1)}, u32[]{:S(2)}, u32[]{:S(2)}) collective-permute-start(bf16[256,256]{1,0:T(8,128)(2,1)S(1)} %get-tuple-element.88.step), channel_id=1, source_target_pairs={{0,12},{1,13},{2,14},{3,15},{4,8},{5,9},{6,10},{7,11},{8,4},{9,5},... | collective-permute-start | bytes 393224 | tf_op jit(solution)/shard_map/ppermute | solution.py:448
  26.7 5.5 %collective-permute-start.6 = (bf16[272,128]{1,0:T(8,128)(2,1)S(1)}, bf16[272,128]{1,0:T(8,128)(2,1)S(1)}, u32[]{:S(2)}, u32[]{:S(2)}) collective-permute-start(bf16[272,128]{1,0:T(8,128)(2,1)S(1)} %get-tuple-element.87.own), channel_id=1, source_target_pairs={{0,12},{1,13},{2,14},{3,15},{4,8},{5,9},{6,10},{7,11},{8,4},{9,5},... | collective-permute-start | bytes 208904 | tf_op jit(solution)/shard_map/ppermute | solution.py:457
  28.2 7.5 %collective-permute-start.9 = (bf16[256,256]{1,0:T(8,128)(2,1)S(1)}, bf16[256,256]{1,0:T(8,128)(2,1)S(1)}, u32[]{:S(2)}, u32[]{:S(2)}) collective-permute-start(bf16[256,256]{1,0:T(8,128)(2,1)S(1)} %get-tuple-element.91.step), channel_id=1, source_target_pairs={{0,16},{1,17},{2,18},{3,19},{4,20},{5,21},{6,22},{7,23},{8,24},{9,... | collective-permute-start | bytes 393224 | tf_op jit(solution)/shard_map/ppermute | solution.py:448
  32.4 3.6 %collective-permute-start.8 = (bf16[272,128]{1,0:T(8,128)(2,1)S(1)}, bf16[272,128]{1,0:T(8,128)(2,1)S(1)}, u32[]{:S(2)}, u32[]{:S(2)}) collective-permute-start(bf16[272,128]{1,0:T(8,128)(2,1)S(1)} %get-tuple-element.90.own), channel_id=1, source_target_pairs={{0,16},{1,17},{2,18},{3,19},{4,20},{5,21},{6,22},{7,23},{8,24},{9,... | collective-permute-start | bytes 208904 | tf_op jit(solution)/shard_map/ppermute | solution.py:457
  33.9 6.3 %collective-permute-start.11 = (bf16[256,256]{1,0:T(8,128)(2,1)S(1)}, bf16[256,256]{1,0:T(8,128)(2,1)S(1)}, u32[]{:S(2)}, u32[]{:S(2)}) collective-permute-start(bf16[256,256]{1,0:T(8,128)(2,1)S(1)} %get-tuple-element.94.step), channel_id=1, source_target_pairs={{0,48},{1,49},{2,50},{3,51},{4,52},{5,53},{6,54},{7,55},{8,56},{9,... | collective-permute-start | bytes 393224 | tf_op jit(solution)/shard_map/ppermute | solution.py:448
  36.4 5.2 %collective-permute-start.10 = (bf16[272,128]{1,0:T(8,128)(2,1)S(1)}, bf16[272,128]{1,0:T(8,128)(2,1)S(1)}, u32[]{:S(2)}, u32[]{:S(2)}) collective-permute-start(bf16[272,128]{1,0:T(8,128)(2,1)S(1)} %get-tuple-element.93.own), channel_id=1, source_target_pairs={{0,48},{1,49},{2,50},{3,51},{4,52},{5,53},{6,54},{7,55},{8,56},{9,... | collective-permute-start | bytes 208904 | tf_op jit(solution)/shard_map/ppermute | solution.py:457
  38.9 4.3 %collective-permute-start.13 = (bf16[256,256]{1,0:T(8,128)(2,1)S(1)}, bf16[256,256]{1,0:T(8,128)(2,1)S(1)}, u32[]{:S(2)}, u32[]{:S(2)}) collective-permute-start(bf16[256,256]{1,0:T(8,128)(2,1)S(1)} %get-tuple-element.97.step), channel_id=1, source_target_pairs={{0,64},{1,65},{2,66},{3,67},{4,68},{5,69},{6,70},{7,71},{8,72},{9,... | collective-permute-start | bytes 393224 | tf_op jit(solution)/shard_map/ppermute | solution.py:448
  41.8 3.4 %collective-permute-start.12 = (bf16[272,128]{1,0:T(8,128)(2,1)S(1)}, bf16[272,128]{1,0:T(8,128)(2,1)S(1)}, u32[]{:S(2)}, u32[]{:S(2)}) collective-permute-start(bf16[272,128]{1,0:T(8,128)(2,1)S(1)} %get-tuple-element.96.own), channel_id=1, source_target_pairs={{0,64},{1,65},{2,66},{3,67},{4,68},{5,69},{6,70},{7,71},{8,72},{9,... | collective-permute-start | bytes 208904 | tf_op jit(solution)/shard_map/ppermute | solution.py:457
  45.5 4.5 %collective-permute-start.14 = (bf16[272,128]{1,0:T(8,128)(2,1)S(1)}, bf16[272,128]{1,0:T(8,128)(2,1)S(1)}, u32[]{:S(2)}, u32[]{:S(2)}) collective-permute-start(bf16[272,128]{1,0:T(8,128)(2,1)S(1)} %get-tuple-element.99.own), channel_id=1, source_target_pairs={{0,192},{1,193},{2,194},{3,195},{4,196},{5,197},{6,198},{7,199},{8... | collective-permute-start | bytes 208904 | tf_op jit(solution)/shard_map/ppermute | solution.py:461
  52.8 7.2 %collective-permute-start.15 = (bf16[272,128]{1,0:T(8,128)(2,1)S(1)}, bf16[272,128]{1,0:T(8,128)(2,1)S(1)}, u32[]{:S(2)}, u32[]{:S(2)}) collective-permute-start(bf16[272,128]{1,0:T(8,128)(2,1)S(1)} %get-tuple-element.104.own), channel_id=1, source_target_pairs={{0,1},{1,0},{2,3},{3,2},{4,5},{5,4},{6,7},{7,6},{8,9},{9,8},{10,11... | collective-permute-start | bytes 208904 | tf_op jit(solution)/shard_map/ppermute | solution.py:457
  60.3 4.1 %collective-permute-start.16 = (bf16[272,128]{1,0:T(8,128)(2,1)S(1)}, bf16[272,128]{1,0:T(8,128)(2,1)S(1)}, u32[]{:S(2)}, u32[]{:S(2)}) collective-permute-start(bf16[272,128]{1,0:T(8,128)(2,1)S(1)} %get-tuple-element.105.own), channel_id=1, source_target_pairs={{0,2},{1,3},{2,0},{3,1},{4,6},{5,7},{6,4},{7,5},{8,10},{9,11},{10,... | collective-permute-start | bytes 208904 | tf_op jit(solution)/shard_map/ppermute | solution.py:457
  64.8 4.9 %collective-permute-start.17 = (bf16[272,128]{1,0:T(8,128)(2,1)S(1)}, bf16[272,128]{1,0:T(8,128)(2,1)S(1)}, u32[]{:S(2)}, u32[]{:S(2)}) collective-permute-start(bf16[272,128]{1,0:T(8,128)(2,1)S(1)} %get-tuple-element.107.own), channel_id=1, source_target_pairs={{0,4},{1,5},{2,6},{3,7},{4,0},{5,1},{6,2},{7,3},{8,12},{9,13},{10,... | collective-permute-start | bytes 208904 | tf_op jit(solution)/shard_map/ppermute | solution.py:457
  70.0 5.4 %collective-permute-start.18 = (bf16[272,128]{1,0:T(8,128)(2,1)S(1)}, bf16[272,128]{1,0:T(8,128)(2,1)S(1)}, u32[]{:S(2)}, u32[]{:S(2)}) collective-permute-start(bf16[272,128]{1,0:T(8,128)(2,1)S(1)} %get-tuple-element.109.own), channel_id=1, source_target_pairs={{0,12},{1,13},{2,14},{3,15},{4,8},{5,9},{6,10},{7,11},{8,4},{9,5},... | collective-permute-start | bytes 208904 | tf_op jit(solution)/shard_map/ppermute | solution.py:457
  75.6 3.2 %collective-permute-start.19 = (bf16[272,128]{1,0:T(8,128)(2,1)S(1)}, bf16[272,128]{1,0:T(8,128)(2,1)S(1)}, u32[]{:S(2)}, u32[]{:S(2)}) collective-permute-start(bf16[272,128]{1,0:T(8,128)(2,1)S(1)} %get-tuple-element.111.own), channel_id=1, source_target_pairs={{0,16},{1,17},{2,18},{3,19},{4,20},{5,21},{6,22},{7,23},{8,24},{9,... | collective-permute-start | bytes 208904 | tf_op jit(solution)/shard_map/ppermute | solution.py:457
  79.2 4.5 %collective-permute-start.20 = (bf16[272,128]{1,0:T(8,128)(2,1)S(1)}, bf16[272,128]{1,0:T(8,128)(2,1)S(1)}, u32[]{:S(2)}, u32[]{:S(2)}) collective-permute-start(bf16[272,128]{1,0:T(8,128)(2,1)S(1)} %get-tuple-element.113.own), channel_id=1, source_target_pairs={{0,48},{1,49},{2,50},{3,51},{4,52},{5,53},{6,54},{7,55},{8,56},{9,... | collective-permute-start | bytes 208904 | tf_op jit(solution)/shard_map/ppermute | solution.py:457
  83.9 3.5 %collective-permute-start.21 = (bf16[272,128]{1,0:T(8,128)(2,1)S(1)}, bf16[272,128]{1,0:T(8,128)(2,1)S(1)}, u32[]{:S(2)}, u32[]{:S(2)}) collective-permute-start(bf16[272,128]{1,0:T(8,128)(2,1)S(1)} %get-tuple-element.115.own), channel_id=1, source_target_pairs={{0,64},{1,65},{2,66},{3,67},{4,68},{5,69},{6,70},{7,71},{8,72},{9,... | collective-permute-start | bytes 208904 | tf_op jit(solution)/shard_map/ppermute | solution.py:457
  87.8 4.7 %collective-permute-start.22 = (bf16[272,128]{1,0:T(8,128)(2,1)S(1)}, bf16[272,128]{1,0:T(8,128)(2,1)S(1)}, u32[]{:S(2)}, u32[]{:S(2)}) collective-permute-start(bf16[272,128]{1,0:T(8,128)(2,1)S(1)} %get-tuple-element.117.own), channel_id=1, source_target_pairs={{0,192},{1,193},{2,194},{3,195},{4,196},{5,197},{6,198},{7,199},{8... | collective-permute-start | bytes 208904 | tf_op jit(solution)/shard_map/ppermute | solution.py:461
  95.3 7.9 %collective-permute-start.23 = (bf16[272,128]{1,0:T(8,128)(2,1)S(1)}, bf16[272,128]{1,0:T(8,128)(2,1)S(1)}, u32[]{:S(2)}, u32[]{:S(2)}) collective-permute-start(bf16[272,128]{1,0:T(8,128)(2,1)S(1)} %get-tuple-element.124.own), channel_id=1, source_target_pairs={{0,1},{1,0},{2,3},{3,2},{4,5},{5,4},{6,7},{7,6},{8,9},{9,8},{10,11... | collective-permute-start | bytes 208904 | tf_op jit(solution)/shard_map/ppermute | solution.py:457
  103.5 4.2 %collective-permute-start.24 = (bf16[272,128]{1,0:T(8,128)(2,1)S(1)}, bf16[272,128]{1,0:T(8,128)(2,1)S(1)}, u32[]{:S(2)}, u32[]{:S(2)}) collective-permute-start(bf16[272,128]{1,0:T(8,128)(2,1)S(1)} %get-tuple-element.125.own), channel_id=1, source_target_pairs={{0,2},{1,3},{2,0},{3,1},{4,6},{5,7},{6,4},{7,5},{8,10},{9,11},{10,... | collective-permute-start | bytes 208904 | tf_op jit(solution)/shard_map/ppermute | solution.py:457
  108.0 4.9 %collective-permute-start.25 = (bf16[272,128]{1,0:T(8,128)(2,1)S(1)}, bf16[272,128]{1,0:T(8,128)(2,1)S(1)}, u32[]{:S(2)}, u32[]{:S(2)}) collective-permute-start(bf16[272,128]{1,0:T(8,128)(2,1)S(1)} %get-tuple-element.127.own), channel_id=1, source_target_pairs={{0,4},{1,5},{2,6},{3,7},{4,0},{5,1},{6,2},{7,3},{8,12},{9,13},{10,... | collective-permute-start | bytes 208904 | tf_op jit(solution)/shard_map/ppermute | solution.py:457
  113.2 5.4 %collective-permute-start.26 = (bf16[272,128]{1,0:T(8,128)(2,1)S(1)}, bf16[272,128]{1,0:T(8,128)(2,1)S(1)}, u32[]{:S(2)}, u32[]{:S(2)}) collective-permute-start(bf16[272,128]{1,0:T(8,128)(2,1)S(1)} %get-tuple-element.129.own), channel_id=1, source_target_pairs={{0,12},{1,13},{2,14},{3,15},{4,8},{5,9},{6,10},{7,11},{8,4},{9,5},... | collective-permute-start | bytes 208904 | tf_op jit(solution)/shard_map/ppermute | solution.py:457
  118.9 3.2 %collective-permute-start.27 = (bf16[272,128]{1,0:T(8,128)(2,1)S(1)}, bf16[272,128]{1,0:T(8,128)(2,1)S(1)}, u32[]{:S(2)}, u32[]{:S(2)}) collective-permute-start(bf16[272,128]{1,0:T(8,128)(2,1)S(1)} %get-tuple-element.131.own), channel_id=1, source_target_pairs={{0,16},{1,17},{2,18},{3,19},{4,20},{5,21},{6,22},{7,23},{8,24},{9,... | collective-permute-start | bytes 208904 | tf_op jit(solution)/shard_map/ppermute | solution.py:457
  122.4 4.5 %collective-permute-start.28 = (bf16[272,128]{1,0:T(8,128)(2,1)S(1)}, bf16[272,128]{1,0:T(8,128)(2,1)S(1)}, u32[]{:S(2)}, u32[]{:S(2)}) collective-permute-start(bf16[272,128]{1,0:T(8,128)(2,1)S(1)} %get-tuple-element.133.own), channel_id=1, source_target_pairs={{0,48},{1,49},{2,50},{3,51},{4,52},{5,53},{6,54},{7,55},{8,56},{9,... | collective-permute-start | bytes 208904 | tf_op jit(solution)/shard_map/ppermute | solution.py:457
  127.2 3.5 %collective-permute-start.29 = (bf16[272,128]{1,0:T(8,128)(2,1)S(1)}, bf16[272,128]{1,0:T(8,128)(2,1)S(1)}, u32[]{:S(2)}, u32[]{:S(2)}) collective-permute-start(bf16[272,128]{1,0:T(8,128)(2,1)S(1)} %get-tuple-element.135.own), channel_id=1, source_target_pairs={{0,64},{1,65},{2,66},{3,67},{4,68},{5,69},{6,70},{7,71},{8,72},{9,... | collective-permute-start | bytes 208904 | tf_op jit(solution)/shard_map/ppermute | solution.py:457
  131.0 4.5 %collective-permute-start.30 = (bf16[272,128]{1,0:T(8,128)(2,1)S(1)}, bf16[272,128]{1,0:T(8,128)(2,1)S(1)}, u32[]{:S(2)}, u32[]{:S(2)}) collective-permute-start(bf16[272,128]{1,0:T(8,128)(2,1)S(1)} %get-tuple-element.137.own), channel_id=1, source_target_pairs={{0,192},{1,193},{2,194},{3,195},{4,196},{5,197},{6,198},{7,199},{8... | collective-permute-start | bytes 208904 | tf_op jit(solution)/shard_map/ppermute | solution.py:461
  137.8 7.8 %collective-permute-start.31 = (f32[1,128]{1,0:T(1,128)S(1)}, f32[1,128]{1,0:T(1,128)S(1)}, u32[]{:S(2)}, u32[]{:S(2)}) collective-permute-start(f32[1,128]{1,0:T(1,128)S(1)} %slice.11), channel_id=1, source_target_pairs={{0,1},{1,0},{2,3},{3,2},{4,5},{5,4},{6,7},{7,6},{8,9},{9,8},{10,11... | collective-permute-start | bytes 1544 | tf_op jit(solution)/shard_map/ppermute | solution.py:473
  (10 other events, 39.9 us)
